TPU v7x, 256 devices: a whole 4x4x8 slice. The times are simulated.
256 devices in a mesh: grp: 32 (over z_hi, x, y), tp: 8 (over z_lo, core).
Axes of the slice: x: 4, y: 4, z: 8 (z_hi: 2, z_lo: 4; z = z_hi * 4 + z_lo), core: 2. Of those that a mesh axis runs over, the one named last changes fastest.
Arguments:
- queries: bfloat16 [3, 32, 24, 4096], P(None, 'grp', None, 'tp'), may hold values from -12 to 12
- fresh_pairs: bfloat16 [3, 32, 24, 2, 1024], P(None, 'grp', None, None, 'tp'), may hold values from -6 to 6
- cache_pool: bfloat16 [32, 80, 2, 128, 1024], P('grp', None, None, None, 'tp'), may hold values from -6 to 6
- out_weight: bfloat16 [4096, 4096], P('tp'), may hold values from -0.8984375 to 0.8984375
- lengths: int32 [32, 24], P('grp'), may hold values from 1 to 509, as said below
- page_table: int32 [32, 24, 4], P('grp'), may hold values from 0 to 79, as said below
- victims: int32 [32, 16], P('grp'), may hold values from 0 to 23, as said below
- victim_dest: int32 [32, 16], replicated, may hold values from 0 to 31, as said below
- section_plan: int32 [32, 16, 3], replicated, may hold values from 0 to 2, as said below
Outputs:
- projected: bfloat16 [32, 24, 3, 4096], P('grp', 'tp')
- migrated: bfloat16 [32, 16, 3, 2, 128, 1024], P('grp', None, None, None, None, 'tp')
Inputs may be any that keep to these rules, and one draw needn't show every extreme that they name: `lengths`: in every group each victim holds between 256 and 381 tokens, and one other request holds exactly 509. `page_table`: the first ceil((lengths + 3) / 128) entries of a request are pool pages that no other request of the group names among its first entries; later entries are unused. `victims`: 16 distinct requests of the group. `victim_dest`: A group's victims go to 16 distinct groups other than itself; for each j, every group is the target of victim j of exactly one source. `section_plan`: for each victim, a permutation of its pages 0 .. 3 - 1 over the steps.
All inputs are finite; a program needn't handle non-finite values.
Results may differ from a plain program's by a relative error of at most 0.0051.
Values may be sent and summed in bfloat16 or wider, within the bound.
No kernel may reach another device: no remote copies, remote signals or barrier semaphores. Data moves between devices by JAX's collectives and lax.ppermute only.
A program may use at most 128 MiB of HBM per device.

v0:
```python
import math

import jax
import jax.numpy as jnp
from jax import lax
from jax.sharding import PartitionSpec as P

HEAD_SIZE = 128


masked_score = -1e30


def attend_all(query_steps, fresh_steps, cache, table, request_lengths, kv_heads, query_heads):
    steps_total, request_list = (query_steps.shape[0], query_steps.shape[1])
    entries = table.shape[1]
    section_span = entries * cache.shape[2]
    key_rows = cache[table, 0].reshape(request_list, section_span, kv_heads, HEAD_SIZE)
    value_rows = cache[table, 1].reshape(request_list, section_span, kv_heads, HEAD_SIZE)
    grouped_heads = query_steps.reshape(
        steps_total, request_list, kv_heads, query_heads // kv_heads, HEAD_SIZE
    )
    fresh_keys = fresh_steps[:, :, 0].reshape(steps_total, request_list, kv_heads, HEAD_SIZE)
    fresh_values = fresh_steps[:, :, 1].reshape(steps_total, request_list, kv_heads, HEAD_SIZE)
    scale = math.sqrt(HEAD_SIZE)
    old_scores = (
        jnp.einsum("srhgd,rkhd->rhgsk", grouped_heads, key_rows, preferred_element_type=jnp.float32)
        / scale
    )
    new_scores = (
        jnp.einsum(
            "srhgd,trhd->rhgst", grouped_heads, fresh_keys, preferred_element_type=jnp.float32
        )
        / scale
    )
    old_visible = jnp.arange(section_span)[None, :] < request_lengths[:, None]
    old_scores = jnp.where(old_visible[:, None, None, None, :], old_scores, masked_score)
    new_visible = jnp.arange(steps_total)[None, :] <= jnp.arange(steps_total)[:, None]
    new_scores = jnp.where(new_visible[None, None, None, :, :], new_scores, masked_score)
    peak = jnp.maximum(
        jnp.max(old_scores, axis=-1, keepdims=True), jnp.max(new_scores, axis=-1, keepdims=True)
    )
    old_weights = jnp.exp(old_scores - peak)
    new_weights = jnp.exp(new_scores - peak)
    total = jnp.sum(old_weights, axis=-1) + jnp.sum(new_weights, axis=-1)
    old_probs = old_weights.astype(jnp.bfloat16)
    new_probs = new_weights.astype(jnp.bfloat16)
    summed = jnp.einsum(
        "rhgsk,rkhd->srhgd", old_probs, value_rows, preferred_element_type=jnp.float32
    )
    summed = summed + jnp.einsum(
        "rhgst,trhd->srhgd", new_probs, fresh_values, preferred_element_type=jnp.float32
    )
    total = jnp.moveaxis(total, 3, 0)[..., None]
    return (
        (summed / total)
        .astype(jnp.bfloat16)
        .reshape(steps_total, request_list, query_heads * HEAD_SIZE)
    )


def local(
    queries,
    fresh_pairs,
    cache_pool,
    out_weight,
    lengths,
    page_table,
    victims,
    victim_dest,
    section_plan,
):
    steps_total = queries.shape[0]
    page_len = cache_pool.shape[3]
    pair_width = cache_pool.shape[4]
    kv_heads = pair_width // HEAD_SIZE
    query_heads = queries.shape[3] // HEAD_SIZE
    victim_count = victims.shape[1]
    groups = lax.axis_size("grp")
    own_group = lax.axis_index("grp")
    cache = cache_pool[0]
    table = page_table[0]
    request_lengths = lengths[0]
    fresh_steps = fresh_pairs[:, 0]
    slots = jnp.arange(victim_count)
    victim_pages = table[victims[0]][:, :steps_total]
    victim_lengths = request_lengths[victims[0]]
    victim_fresh = fresh_steps[:, victims[0]]
    own_dest = lax.dynamic_index_in_dim(victim_dest, own_group, 0, keepdims=False)
    own_plan = lax.dynamic_index_in_dim(section_plan, own_group, 0, keepdims=False)
    send_map = (own_dest[None, :] == jnp.arange(groups)[:, None]).astype(jnp.bfloat16)
    incoming_flags = (victim_dest == own_group).astype(jnp.int32)
    receive_map = incoming_flags.astype(jnp.bfloat16)
    page_size = 2 * page_len * pair_width
    migrated = jnp.zeros((victim_count, steps_total, page_size), jnp.bfloat16)
    attended = attend_all(
        queries[:, 0], fresh_steps, cache, table, request_lengths, kv_heads, query_heads
    )
    snapshots = []
    for section_index in range(steps_total):
        picked = own_plan[:, section_index]
        content = cache[victim_pages[slots, picked]]
        offsets = (
            picked[:, None] * page_len + jnp.arange(page_len)[None, :] - victim_lengths[:, None]
        )
        for written in range(section_index + 1):
            hit = (offsets == written)[:, None, :, None]
            content = jnp.where(hit, victim_fresh[written][:, :, None, :], content)
        content = content.reshape(victim_count, page_size)
        snapshots.append(content)
    sectioned = jnp.stack(snapshots, axis=1)
    outgoing = jnp.einsum(
        "gv,vsx->gsx", send_map, sectioned, preferred_element_type=jnp.float32
    ).astype(jnp.bfloat16)
    incoming = lax.all_to_all(outgoing, "grp", split_axis=0, concat_axis=0, tiled=True)
    arrived = jnp.einsum(
        "gv,gsx->vsx", receive_map, incoming, preferred_element_type=jnp.float32
    ).astype(jnp.bfloat16)
    for section_index in range(steps_total):
        place_arrived = arrived[:, section_index]
        page_now = jnp.sum(incoming_flags * section_plan[:, :, section_index], axis=0)
        target_hit = page_now[:, None] == jnp.arange(steps_total)[None, :]
        migrated = jnp.where(target_hit[:, :, None], place_arrived[:, None, :], migrated)
    stacked = jnp.moveaxis(attended, 0, 1)
    projected = lax.psum_scatter(
        jnp.einsum("rsk,kd->rsd", stacked, out_weight, preferred_element_type=jnp.float32),
        "tp",
        scatter_dimension=0,
        tiled=True,
    )
    projected = projected.astype(jnp.bfloat16)[None]
    migrated = migrated.reshape(1, victim_count, steps_total, 2, page_len, pair_width)
    return (projected, migrated)


def solution(mesh):
    return jax.shard_map(
        local,
        mesh=mesh,
        in_specs=(
            P(None, "grp", None, "tp"),
            P(None, "grp", None, None, "tp"),
            P("grp", None, None, None, "tp"),
            P("tp", None),
            P("grp", None),
            P("grp", None, None),
            P("grp", None),
            P(),
            P(),
        ),
        out_specs=(P("grp", "tp", None, None), P("grp", None, None, None, None, "tp")),
        check_vma=False,
    )
```

profile of v0, /device:TPU:12, one launch (start us, length us, event | category | flops | bytes accessed | tf_op | source)
XLA Modules:
  0.0 337.3 jit_solution(658231084776135524)
XLA Ops:
  0.6 1.0 dynamic-slice_reduce_fusion
  1.6 0.7 multiply_bitcast_fusion.2
  2.3 0.8 copy.44
  3.0 1.3 gather_fusion.2
  4.3 0.6 gather_fusion.4
  4.9 0.7 gather_fusion.9
  5.6 0.7 gather_fusion.5
  6.3 3.2 gather_fusion.10
  9.5 3.2 gather_fusion.6
  12.8 0.7 gather_fusion.7
  13.5 3.2 gather_fusion.8
  16.7 0.6 gather_fusion.3
  17.6 4.3 %select_select_fusion.2 = (bf16[16,2,128,128]{3,2,1,0:T(8,128)(2,1)}, bf16[16,2,128,128]{3,2,1,0:T(8,128)(2,1)}, bf16[16,2,128,128]{3,2,1,0:T(8,128)(2,1)}) fusion(bf16[16,2,128,128]{3,2,1,0:T(8,128)(2,1)S(1)} %gather_fusion.8, pred[16,128]{1,0:T(8,128)(4,1)S(1)} %get-tuple-element.30, pred[16,128]{1,0:T(8,128)(4,1)S(1)} %get-tuple-element.29, ...), kind=kLoop, calls=%fused_computation.38 | loop fusion | flops 3145728 | bytes 6328320 | tf_op jit(solution)/shard_map/jit(_where)/select_n | solution.py:108
  21.9 1.5 select_n.198
  23.4 1.5 select_n.203
  25.0 1.5 select_n.209
  26.7 3.8 %convolution_convert_fusion = bf16[32,3,32768]{2,0,1:T(8,128)(2,1)} fusion(bf16[16,1,32768]{2,0,1:T(8,128)(2,1)S(1)} %select_n.209, bf16[16,1,32768]{2,0,1:T(8,128)(2,1)S(1)} %select_n.203, bf16[16,1,32768]{2,0,1:T(8,128)(2,1)S(1)} %select_n.198, s32[16]{0:T(128)S(1)} %dynamic-slice_reduce_fusion.1), kind=kOutput, calls=%fused_computation.11 | convolution fusion | flops 113246720 | bytes 9437248 | tf_op jit(solution)/shard_map/gv,vsx->gsx/dot_general | solution.py:112
  30.5 11.4 %copy.49 = bf16[32,3,32768]{2,1,0:T(4,128)(2,1)} copy(bf16[32,3,32768]{2,0,1:T(8,128)(2,1)} %convolution_convert_fusion) | data formatting | bytes 12582912 | tf_op jit(solution)/shard_map/convert_element_type | solution.py:114
  41.9 14.3 %all-to-all-start = ((bf16[32,3,32768]{2,1,0:T(4,128)(2,1)}), bf16[32,3,32768]{2,1,0:T(4,128)(2,1)}, u32[]{:S(2)}, u32[]{:S(2)}) async-start(bf16[32,3,32768]{2,1,0:T(4,128)(2,1)} %copy.49), calls=%async_computation | async-start | bytes 16777216 | tf_op jit(solution)/shard_map/all_to_all | solution.py:115
  56.5 5.6 %gather_fusion.1 = bf16[96,128,128]{2,1,0:T(8,128)(2,1)} fusion(bf16[80,2,128,128]{3,2,1,0:T(8,128)(2,1)} %bitcast.178, s32[96]{0:T(128)S(1)} %reshape.663), kind=kCustom, calls=%fused_computation.1 | custom fusion | bytes 6292224 | tf_op jit(solution)/shard_map/gather | solution.py:18
  62.3 4.0 %gather_fusion = bf16[96,128,128]{2,1,0:T(8,128)(2,1)S(1)} fusion(bf16[80,2,128,128]{3,2,1,0:T(8,128)(2,1)} %bitcast.179, s32[96]{0:T(128)S(1)} %reshape.657), kind=kCustom, calls=%fused_computation | custom fusion | bytes 6292224 | tf_op jit(solution)/shard_map/gather | solution.py:19
  66.4 0.6 fusion.64
  67.0 2.9 fusion.63
  70.1 0.4 fusion.16
  70.6 0.3 convolution_bitcast_fusion
  70.8 0.7 fusion.12
  71.7 3.1 fusion.1
  74.7 0.6 dynamic-slice
  76.0 247.1 %all-reduce.4 = bf16[24,3,4096]{2,0,1:T(8,128)(2,1)S(1)} all-reduce(f32[24,3,4096]{2,0,1:T(8,128)S(1)} %fusion.1), channel_id=2, replica_groups=mesh['grp'=32,'tp'=8] {'tp'}, use_global_device_ids=true, to_apply=%region_4.5.clone | all-reduce | flops 294912 | bytes 1769472
  323.2 0.7 copy.51
  324.2 10.2 %convolution_convert_fusion.1 = bf16[16,3,32768]{2,0,1:T(8,128)(2,1)S(1)} fusion(bf16[32,3,32768]{2,1,0:T(4,128)(2,1)} %all-to-all-done, pred[32,16]{0,1:T(8,128)(4,1)S(1)} %get-tuple-element.11), kind=kOutput, calls=%fused_computation.12 | convolution fusion | flops 102237184 | bytes 9437696 | tf_op jit(solution)/shard_map/gv,gsx->vsx/dot_general | solution.py:116
  335.2 2.1 select_select_fusion
  (53 shorter events, 2.3 us)
Async XLA Ops:
  6.3 10.4 %copy-start.3 = (bf16[3,1,24,2,128]{4,3,2,1,0:T(2,128)(2,1)S(1)}, bf16[3,1,24,2,128]{4,3,2,1,0:T(2,128)(2,1)}, u32[]{:S(2)}) copy-start(bf16[3,1,24,2,128]{4,3,2,1,0:T(2,128)(2,1)} %param.10) | copy-start | bytes 110596
  21.9 4.6 %copy-start.4 = (s32[32,16]{0,1:T(8,128)S(1)}, s32[32,16]{0,1:T(8,128)}, u32[]{:S(2)}) copy-start(s32[32,16]{0,1:T(8,128)} %param.16) | copy-start | bytes 6148
  41.9 14.3 %copy-start.5 = (s32[1,24,4]{1,2,0:T(4,128)S(1)}, s32[1,24,4]{1,2,0:T(4,128)}, u32[]{:S(2)}) copy-start(s32[1,24,4]{1,2,0:T(4,128)} %param.14) | copy-start | bytes 1156
  41.9 282.3 %all-to-all-start = ((bf16[32,3,32768]{2,1,0:T(4,128)(2,1)}), bf16[32,3,32768]{2,1,0:T(4,128)(2,1)}, u32[]{:S(2)}, u32[]{:S(2)}) async-start(bf16[32,3,32768]{2,1,0:T(4,128)(2,1)} %copy.49), calls=%async_computation | async-start | bytes 16777216 | tf_op jit(solution)/shard_map/all_to_all | solution.py:115
  56.4 5.6 %copy-start.2 = (bf16[3,1,24,512]{3,2,1,0:T(8,128)(2,1)S(1)}, bf16[3,1,24,512]{3,2,1,0:T(8,128)(2,1)}, u32[]{:S(2)}) copy-start(bf16[3,1,24,512]{3,2,1,0:T(8,128)(2,1)} %param.9) | copy-start | bytes 221188
  62.3 4.1 %copy-start = (s32[1,24]{1,0:T(1,128)S(1)}, s32[1,24]{1,0:T(1,128)}, u32[]{:S(2)}) copy-start(s32[1,24]{1,0:T(1,128)} %param.13) | copy-start | bytes 292
  71.6 3.2 copy-start.6
  71.6 252.2 %copy-start.1 = (s32[32,16,3]{0,1,2:T(8,128)S(1)}, s32[32,16,3]{0,1,2:T(8,128)}, u32[]{:S(2)}) copy-start(s32[32,16,3]{0,1,2:T(8,128)} %param.17) | copy-start | bytes 18436
where the time goes:
time: 338 us; the launch traced here: 337 us
  blocking collectives  247 us (73%)
  local copies, waits for them, and re-layouts  44.4 us (13%)
  matrix products  21.7 us (6%)
  starting transfers between devices  14.3 us (4%)
  other arithmetic  8.17 us (2%)
    unnamed x1, blocking collectives  247 us
    all_to_all x1, starting transfers between devices, local(): lax.all_to_all(outgoing, 'grp', split_axis=0, concat_axis=0, tiled=True)  14.3 us
    gather x6, local copies, waits for them, and re-layouts, local(): content = cache[victim_pages[slots, picked]]  11.7 us
    convert_element_type x1, local copies, waits for them, and re-layouts, local(): outgoing = jnp.einsum('gv,vsx->gsx', send_map, sectioned, preferred_eleme...  11.4 us
    dot_general x1, matrix products, local(): jnp.einsum('gv,gsx->vsx', receive_map, incoming, preferred_element_type=j...  10.2 us
  transfers between devices with their start and end apart: 1, of which 0 were waited for; matrix products, arithmetic and copies ran while one was open for 6% of the time, Pallas kernels for 0%

commit v1 on v0

v1 whole, which is shorter than its diff:
```python
import math

import jax
import jax.numpy as jnp
from jax import lax
from jax.experimental import pallas as pl
from jax.experimental.pallas import tpu as pltpu
from jax.sharding import PartitionSpec as P

HEAD_SIZE = 128
HALVES = 2
STRAIGHT = 8
LIFTED = 2


masked_score = -1e30


def attend_all(query_steps, fresh_steps, cache, table, request_lengths, kv_heads, query_heads):
    steps_total, request_list = (query_steps.shape[0], query_steps.shape[1])
    entries = table.shape[1]
    section_span = entries * cache.shape[2]
    key_rows = cache[table, 0].reshape(request_list, section_span, kv_heads, HEAD_SIZE)
    value_rows = cache[table, 1].reshape(request_list, section_span, kv_heads, HEAD_SIZE)
    grouped_heads = query_steps.reshape(
        steps_total, request_list, kv_heads, query_heads // kv_heads, HEAD_SIZE
    )
    fresh_keys = fresh_steps[:, :, 0].reshape(steps_total, request_list, kv_heads, HEAD_SIZE)
    fresh_values = fresh_steps[:, :, 1].reshape(steps_total, request_list, kv_heads, HEAD_SIZE)
    scale = math.sqrt(HEAD_SIZE)
    old_scores = (
        jnp.einsum("srhgd,rkhd->rhgsk", grouped_heads, key_rows, preferred_element_type=jnp.float32)
        / scale
    )
    new_scores = (
        jnp.einsum(
            "srhgd,trhd->rhgst", grouped_heads, fresh_keys, preferred_element_type=jnp.float32
        )
        / scale
    )
    old_visible = jnp.arange(section_span)[None, :] < request_lengths[:, None]
    old_scores = jnp.where(old_visible[:, None, None, None, :], old_scores, masked_score)
    new_visible = jnp.arange(steps_total)[None, :] <= jnp.arange(steps_total)[:, None]
    new_scores = jnp.where(new_visible[None, None, None, :, :], new_scores, masked_score)
    peak = jnp.maximum(
        jnp.max(old_scores, axis=-1, keepdims=True), jnp.max(new_scores, axis=-1, keepdims=True)
    )
    old_weights = jnp.exp(old_scores - peak)
    new_weights = jnp.exp(new_scores - peak)
    total = jnp.sum(old_weights, axis=-1) + jnp.sum(new_weights, axis=-1)
    old_probs = old_weights.astype(jnp.bfloat16)
    new_probs = new_weights.astype(jnp.bfloat16)
    summed = jnp.einsum(
        "rhgsk,rkhd->srhgd", old_probs, value_rows, preferred_element_type=jnp.float32
    )
    summed = summed + jnp.einsum(
        "rhgst,trhd->srhgd", new_probs, fresh_values, preferred_element_type=jnp.float32
    )
    total = jnp.moveaxis(total, 3, 0)[..., None]
    return (
        (summed / total)
        .astype(jnp.bfloat16)
        .reshape(steps_total, request_list, query_heads * HEAD_SIZE)
    )


def route(own_ref, cross_ref, count_ref, via_ref, half, plane, straight):
    def source(i, carry):
        s = half * plane + i

        def pick(_, state):
            free, chosen, once, twice, bad = state
            empty = free & ~once
            pool = jnp.where(empty != 0, empty, free & ~twice)
            bit = pool & -pool
            twice = twice | (once & bit)
            return free & ~bit, chosen | bit, once | bit, twice, bad | (bit == 0).astype(jnp.int32)

        once, twice, bad = carry
        free = cross_ref[s] & ~own_ref[s]
        extra = jnp.maximum(count_ref[s] - straight, 0)
        _, chosen, once, twice, bad = lax.fori_loop(
            0, extra, pick, (free, jnp.int32(0), once, twice, bad)
        )
        via_ref[s] = chosen
        return once, twice, bad

    zero = jnp.int32(0)
    return lax.fori_loop(0, plane, source, (zero, zero, zero))[2]


def goes_via(via_ref, source, place):
    return ((via_ref[source] >> place) & 1) == 1


def first_pages_kernel(
    me_ref,
    own_ref,
    cross_ref,
    count_ref,
    table_ref,
    victim_ref,
    dest_ref,
    cache_ref,
    early_ref,
    via_ref,
    held,
    in_sem,
    out_sem,
):
    count, pages = held.shape[:2]
    groups = dest_ref.shape[1]
    plane = groups // HALVES
    straight = early_ref.shape[0]
    group = me_ref[0]
    my_half = group // plane

    def page_in(j, p):
        page = table_ref[p, victim_ref[0, j]]
        return pltpu.make_async_copy(cache_ref.at[page], held.at[j, p], in_sem.at[j])

    def copy_out(j, rank):
        return pltpu.make_async_copy(held.at[j], early_ref.at[rank], out_sem)

    def visit(act):
        rank = jnp.int32(0)
        for j in range(count):
            target = dest_ref[j, group]
            leaves = ((target // plane) != my_half) & jnp.logical_not(
                goes_via(via_ref, group, target % plane)
            )
            leaves = leaves & (rank < straight)

            @pl.when(leaves)
            def _():
                act(j, rank)

            rank = rank + jnp.where(leaves, 1, 0)

    def read(j, rank):
        for p in range(pages):
            page_in(j, p).start()

    def write(j, rank):
        for p in range(pages):
            page_in(j, p).wait()
        copy_out(j, rank).start()

    bad = route(own_ref, cross_ref, count_ref, via_ref, my_half, plane, straight)
    visit(read)
    bad = bad | route(own_ref, cross_ref, count_ref, via_ref, 1 - my_half, plane, straight)
    via_ref[groups] = bad
    visit(write)
    visit(lambda j, rank: copy_out(j, rank).wait())


def first_pages(straight, me, masks, table, victims, dest, cache, pages):
    count = victims.shape[1]
    groups = dest.shape[1]
    smem = pl.BlockSpec(memory_space=pltpu.SMEM)
    anywhere = pl.BlockSpec(memory_space=pl.ANY)
    return pl.pallas_call(
        first_pages_kernel,
        out_shape=(
            jax.ShapeDtypeStruct((straight, pages) + cache.shape[1:], cache.dtype),
            jax.ShapeDtypeStruct((groups + 1,), jnp.int32),
        ),
        in_specs=[smem] * 7 + [anywhere],
        out_specs=(anywhere, smem),
        scratch_shapes=[
            pltpu.VMEM((count, pages) + cache.shape[1:], cache.dtype),
            pltpu.SemaphoreType.DMA((count,)),
            pltpu.SemaphoreType.DMA,
        ],
        name="first_pages",
    )(me, *masks, table, victims, dest, cache)


def pack_kernel(
    me_ref,
    via_ref,
    length_ref,
    table_ref,
    victim_ref,
    dest_ref,
    plan_ref,
    fresh_ref,
    cache_ref,
    _,
    own_ref,
    late_ref,
    held,
    in_sem,
    out_sem,
):
    count, pages, rows, _ = held.shape
    steps = fresh_ref.shape[0]
    page_len = rows // 2
    plane = own_ref.shape[0]
    straight = late_ref.shape[0]
    group = me_ref[0]
    my_half = group // plane

    def page_in(j, p):
        page = table_ref[p, victim_ref[0, j]]
        return pltpu.make_async_copy(cache_ref.at[page], held.at[j, p], in_sem.at[j])

    def send(j, rank, act):
        target = dest_ref[j, group]
        place = target % plane
        in_half = ((target // plane) == my_half) | goes_via(via_ref, group, place)
        leaves = jnp.logical_not(in_half) & (rank < straight)

        @pl.when(in_half)
        def _():
            act(pltpu.make_async_copy(held.at[j], own_ref.at[place], out_sem))

        @pl.when(leaves)
        def _():
            act(pltpu.make_async_copy(held.at[j, pages - 1], late_ref.at[rank], out_sem))

        return rank + jnp.where(leaves, 1, 0)

    for j in range(count):
        for p in range(pages):
            page_in(j, p).start()
    row_ids = lax.broadcasted_iota(jnp.int32, (page_len, HEAD_SIZE), 0)
    rank = jnp.int32(0)
    for j in range(count):
        for p in range(pages):
            page_in(j, p).wait()
        victim = victim_ref[0, j]
        first = length_ref[0, victim] - (pages - 1) * page_len
        last_step = jnp.int32(0)
        for s in range(steps):
            last_step = jnp.where(plan_ref[s * count + j, group] == pages - 1, s, last_step)
        for side in range(2):
            span = pl.ds(side * page_len, page_len)
            content = held[j, pages - 1, span, :].astype(jnp.float32)
            for t in range(steps):
                row = jnp.where(t <= last_step, first + t, -1)
                token = fresh_ref[t, victim].astype(jnp.float32)[side : side + 1]
                content = jnp.where(row_ids == row, token, content)
            held[j, pages - 1, span, :] = content.astype(jnp.bfloat16)
        rank = send(j, rank, lambda copy: copy.start())
    rank = jnp.int32(0)
    for j in range(count):
        rank = send(j, rank, lambda copy: copy.wait())


def pack(straight, scalars, fresh, cache, plane, early):
    count = scalars[4].shape[1]
    steps = fresh.shape[0]
    rows, width = cache.shape[1:]
    smem = pl.BlockSpec(memory_space=pltpu.SMEM)
    anywhere = pl.BlockSpec(memory_space=pl.ANY)
    return pl.pallas_call(
        pack_kernel,
        out_shape=(
            jax.ShapeDtypeStruct((plane, steps, rows, width), cache.dtype),
            jax.ShapeDtypeStruct((straight, rows, width), cache.dtype),
        ),
        in_specs=[smem] * 7 + [pl.BlockSpec(memory_space=pltpu.VMEM), anywhere, anywhere],
        out_specs=(anywhere,) * 2,
        scratch_shapes=[
            pltpu.VMEM((count, steps, rows, width), cache.dtype),
            pltpu.SemaphoreType.DMA((count,)),
            pltpu.SemaphoreType.DMA,
        ],
        name="pack_pages",
    )(*scalars, fresh, cache, early)


def relay_kernel(me_ref, via_ref, dest_ref, got_ref, slots_ref, sem):
    plane = slots_ref.shape[0]
    count = dest_ref.shape[0]
    straight = got_ref.shape[0]
    group = me_ref[0]
    my_half = group // plane
    partner = jnp.where(group < plane, group + plane, group - plane)

    def visit(act):
        rank = jnp.int32(0)
        for j in range(count):
            target = dest_ref[j, partner]
            place = target % plane
            came = ((target // plane) == my_half) & jnp.logical_not(
                goes_via(via_ref, partner, place)
            )
            came = came & (rank < straight)

            @pl.when(came)
            def _():
                act(pltpu.make_async_copy(got_ref.at[rank], slots_ref.at[place], sem))

            rank = rank + jnp.where(came, 1, 0)

    visit(lambda copy: copy.start())
    visit(lambda copy: copy.wait())


def relay(me, via, dest, got, plane):
    smem = pl.BlockSpec(memory_space=pltpu.SMEM)
    return pl.pallas_call(
        relay_kernel,
        out_shape=jax.ShapeDtypeStruct((plane,) + got.shape[1:], got.dtype),
        in_specs=[smem, smem, smem, pl.BlockSpec(memory_space=pltpu.VMEM)],
        out_specs=pl.BlockSpec(memory_space=pl.ANY),
        scratch_shapes=[pltpu.SemaphoreType.DMA],
        name="relay_pages",
    )(me, via, dest, got)


def lift_kernel(me_ref, via_ref, own_ref, lifted_ref, sem):
    plane = own_ref.shape[0]
    room = lifted_ref.shape[0]
    group = me_ref[0]
    base = (group // plane) * plane
    place = group % plane

    def visit(act):
        rank = jnp.int32(0)
        for i in range(plane):
            lifted = goes_via(via_ref, base + i, place) & (rank < room)

            @pl.when(lifted)
            def _():
                act(pltpu.make_async_copy(own_ref.at[i], lifted_ref.at[rank], sem))

            rank = rank + jnp.where(lifted, 1, 0)

    visit(lambda copy: copy.start())
    visit(lambda copy: copy.wait())


def lift(me, via, own):
    smem = pl.BlockSpec(memory_space=pltpu.SMEM)
    return pl.pallas_call(
        lift_kernel,
        out_shape=jax.ShapeDtypeStruct((LIFTED,) + own.shape[1:], own.dtype),
        in_specs=[smem, smem, pl.BlockSpec(memory_space=pltpu.VMEM)],
        out_specs=pl.BlockSpec(memory_space=pl.ANY),
        scratch_shapes=[pltpu.SemaphoreType.DMA],
        name="lift_pages",
    )(me, via, own)


def place_early_kernel(me_ref, via_ref, source_ref, own_ref, early_ref, out_ref, sem):
    plane = own_ref.shape[0]
    count, pages = out_ref.shape[:2]
    group = me_ref[0]
    my_half = group // plane

    def visit(act):
        for j in range(count):
            source = source_ref[j]
            near = (source // plane) == my_half
            far = jnp.logical_not(near | goes_via(via_ref, source, group % plane))
            place = source % plane

            @pl.when(near)
            def _():
                act(pltpu.make_async_copy(own_ref.at[place], out_ref.at[j], sem))

            @pl.when(far)
            def _():
                act(
                    pltpu.make_async_copy(
                        early_ref.at[place], out_ref.at[j, pl.ds(0, pages - 1)], sem
                    )
                )

    visit(lambda copy: copy.start())
    visit(lambda copy: copy.wait())


def place_late_kernel(
    me_ref, via_ref, source_ref, late_ref, lifted_ref, _, out_ref, rank_ref, sem
):
    plane = late_ref.shape[0]
    room = lifted_ref.shape[0]
    count, pages = out_ref.shape[:2]
    group = me_ref[0]
    my_half = group // plane
    other = (1 - my_half) * plane
    rank = jnp.int32(0)
    for i in range(plane):
        rank_ref[i] = jnp.minimum(rank, room - 1)
        rank = rank + jnp.where(goes_via(via_ref, other + i, group % plane), 1, 0)

    def visit(act):
        for j in range(count):
            source = source_ref[j]
            place = source % plane
            cross = (source // plane) != my_half
            lifted = cross & goes_via(via_ref, source, group % plane)
            far = cross & jnp.logical_not(lifted)

            @pl.when(far)
            def _():
                act(pltpu.make_async_copy(late_ref.at[place], out_ref.at[j, pages - 1], sem))

            @pl.when(lifted)
            def _():
                act(pltpu.make_async_copy(lifted_ref.at[rank_ref[place]], out_ref.at[j], sem))

    visit(lambda copy: copy.start())
    visit(lambda copy: copy.wait())


def place_early(me, via, sources, own, early):
    smem = pl.BlockSpec(memory_space=pltpu.SMEM)
    vmem = pl.BlockSpec(memory_space=pltpu.VMEM)
    return pl.pallas_call(
        place_early_kernel,
        out_shape=jax.ShapeDtypeStruct((sources.shape[0],) + own.shape[1:], own.dtype),
        in_specs=[smem, smem, smem, vmem, vmem],
        out_specs=pl.BlockSpec(memory_space=pl.ANY),
        scratch_shapes=[pltpu.SemaphoreType.DMA],
        name="place_early",
    )(me, via, sources, own, early)


def place_late(me, via, sources, late, lifted, out):
    smem = pl.BlockSpec(memory_space=pltpu.SMEM)
    vmem = pl.BlockSpec(memory_space=pltpu.VMEM)
    anywhere = pl.BlockSpec(memory_space=pl.ANY)
    return pl.pallas_call(
        place_late_kernel,
        out_shape=jax.ShapeDtypeStruct(out.shape, out.dtype),
        in_specs=[smem, smem, smem, vmem, vmem, anywhere],
        out_specs=anywhere,
        scratch_shapes=[pltpu.SMEM((late.shape[0],), jnp.int32), pltpu.SemaphoreType.DMA],
        input_output_aliases={5: 0},
        name="place_late",
    )(me, via, sources, late, lifted, out)


def local(
    queries,
    fresh_pairs,
    cache_pool,
    out_weight,
    lengths,
    page_table,
    victims,
    victim_dest,
    section_plan,
):
    steps_total = queries.shape[0]
    pool_pages, _, page_len, pair_width = cache_pool.shape[1:]
    kv_heads = pair_width // HEAD_SIZE
    query_heads = queries.shape[3] // HEAD_SIZE
    victim_count = victims.shape[1]
    groups = lax.axis_size("grp")
    ranks = lax.axis_size("tp")
    plane = groups // HALVES
    own_group = lax.axis_index("grp")
    core = lax.axis_index("tp") % 2
    chip = lax.axis_index("tp") // 2
    fresh_steps = fresh_pairs[:, 0]
    pages = cache_pool.reshape(pool_pages, 2 * page_len, pair_width)
    dest = victim_dest.T
    table = page_table[0].T
    plan = section_plan.transpose(2, 1, 0).reshape(steps_total * victim_count, groups)
    sources = jnp.sum(
        jnp.where(dest == own_group, jnp.arange(groups)[None, :], 0), axis=1
    ).astype(jnp.int32)
    me = own_group.astype(jnp.int32)[None]
    half_groups = [list(range(h * plane, (h + 1) * plane)) for h in range(HALVES)]
    swap_halves = [(g, (g + plane) % groups) for g in range(groups)]
    swap_cores = [(r, r ^ 1) for r in range(ranks)]
    chips = ranks // 2
    crossing = (dest // plane) != (jnp.arange(groups) // plane)[None, :]
    bits = jnp.left_shift(jnp.int32(1), dest % plane)
    masks = (
        jnp.sum(jnp.where(crossing, 0, bits), axis=0),
        jnp.sum(jnp.where(crossing, bits, 0), axis=0),
        jnp.sum(crossing.astype(jnp.int32), axis=0),
    )

    def in_half(slots):
        return lax.all_to_all(slots, "grp", 0, 0, axis_index_groups=half_groups, tiled=True)

    def swap(slots):
        return lax.ppermute(slots, "grp", swap_halves)

    def pack_args(via):
        return (me, via, lengths, table, victims, dest, plan)

    early, via = first_pages(STRAIGHT, me, masks, table, victims, dest, pages, steps_total - 1)
    early_got = swap(early)
    own, late = pack(STRAIGHT, pack_args(via), fresh_steps, pages, plane, early)
    own_got = in_half(own)
    attended = attend_all(
        queries[:, 0],
        fresh_steps,
        cache_pool[0],
        page_table[0],
        lengths[0],
        kv_heads,
        query_heads,
    )
    stacked = jnp.moveaxis(attended, 0, 1)
    partial = jnp.einsum("rsk,kd->rsd", stacked, out_weight, preferred_element_type=jnp.float32)
    by_core = partial.reshape((chips, 2, -1) + partial.shape[1:])
    kept = lax.dynamic_index_in_dim(by_core, core, 1, keepdims=False)
    given = lax.dynamic_index_in_dim(by_core, 1 - core, 1, keepdims=False)
    on_chip = kept + lax.ppermute(given, "tp", swap_cores)
    projected = lax.dynamic_index_in_dim(on_chip, chip, 0, keepdims=False)
    on_chip = on_chip.astype(jnp.bfloat16)
    for shift in range(1, chips):
        share = lax.dynamic_index_in_dim(on_chip, (chip + shift) % chips, 0, keepdims=False)
        share = lax.ppermute(
            share, "tp", [(r, (r + 2 * shift) % ranks) for r in range(ranks)]
        )
        projected = projected + share.astype(jnp.float32)
    projected = projected.astype(jnp.bfloat16)

    late, on_chip = lax.optimization_barrier((late, on_chip))
    late_got = swap(late)
    early_slots = relay(me, via, dest, early_got, plane)
    early_slots, own_got = lax.optimization_barrier((early_slots, own_got))
    early_arrived = in_half(early_slots)
    lifted = lift(me, via, own_got)
    lifted, early_arrived = lax.optimization_barrier((lifted, early_arrived))
    lifted_got = swap(lifted)
    migrated = place_early(me, via, sources, own_got, early_arrived)
    late_slots = relay(me, via, dest, late_got, plane)
    late_slots, early_arrived = lax.optimization_barrier((late_slots, early_arrived))
    late_arrived = in_half(late_slots)
    migrated = place_late(me, via, sources, late_arrived, lifted_got, migrated)

    def straight_only(carry):
        no_via = jnp.zeros_like(via)
        early, _ = first_pages(
            victim_count, me, masks, table, victims, dest, pages, steps_total - 1
        )
        own, late = pack(victim_count, pack_args(no_via), fresh_steps, pages, plane, early)
        own_got = in_half(own)
        early_arrived = in_half(relay(me, no_via, dest, swap(early), plane))
        late_arrived = in_half(relay(me, no_via, dest, swap(late), plane))
        out = place_early(me, no_via, sources, own_got, early_arrived)
        lifted = jnp.zeros((LIFTED,) + own.shape[1:], own.dtype)
        return jnp.int32(0), place_late(me, no_via, sources, late_arrived, lifted, out)

    _, migrated = lax.while_loop(lambda c: c[0] > 0, straight_only, (via[groups], migrated))
    migrated = migrated.reshape(1, victim_count, steps_total, 2, page_len, pair_width)
    return (projected[None], migrated)


def solution(mesh):
    return jax.shard_map(
        local,
        mesh=mesh,
        in_specs=(
            P(None, "grp", None, "tp"),
            P(None, "grp", None, None, "tp"),
            P("grp", None, None, None, "tp"),
            P("tp", None),
            P("grp", None),
            P("grp", None, None),
            P("grp", None),
            P(),
            P(),
        ),
        out_specs=(P("grp", "tp", None, None), P("grp", None, None, None, None, "tp")),
        check_vma=False,
    )
```

time: 338 us -> 141 us (0.42)
  blocking collectives: 247 us -> 0 us
  waiting for transfers between devices: 0.01 us -> 38.6 us
  starting transfers between devices: 14.3 us -> 39.6 us
  Pallas kernels: 0 us -> 22.9 us
  local copies, waits for them, and re-layouts: 44.4 us -> 23.2 us
  matrix products: 21.7 us -> 8.87 us
    unnamed x1 -> x0, blocking collectives: 247 us -> none
    ppermute x0 -> x7, waiting for transfers between devices: none -> 34.6 us  [the longest x3 34.6 us: swap(): return lax.ppermute(slots, 'grp', swap_halves)]
    pallas_call x0 -> x7, Pallas kernels: none -> 22.9 us  [the longest x1 6.33 us: place_early(): pl.pallas_call(place_early_kernel, out_shape=jax.ShapeDtypeStruct((source...]
    ppermute x0 -> x7, starting transfers between devices: none -> 16 us  [the longest x3 12.5 us: swap(): return lax.ppermute(slots, 'grp', swap_halves)]
    gather x9 -> x0, local copies, waits for them, and re-layouts: 14.2 us -> none  [the longest x6 11.7 us: local(): content = cache[victim_pages[slots, picked]]]
    dot_general x2 -> x0, matrix products: 14.1 us -> none  [the longest x1 10.2 us: local(): jnp.einsum('gv,gsx->vsx', receive_map, incoming, preferred_element_type=j...]
    convert_element_type x1 -> x0, local copies, waits for them, and re-layouts: 11.4 us -> none  [local(): outgoing = jnp.einsum('gv,vsx->gsx', send_map, sectioned, preferred_eleme...]
    all_to_all x1 -> x3, starting transfers between devices: 14.3 us -> 23.7 us  [in_half(): lax.all_to_all(slots, 'grp', 0, 0, axis_index_groups=half_groups, tiled=T...]
  transfers between devices with their start and end apart: 1 -> 10, of which waited for: 0 -> 4; matrix products, arithmetic and copies ran while one was open for 6% -> 24% of each run, Pallas kernels for 0% -> 12%
where the time goes in v1:
time: 141 us; the launch traced here: 140 us
  starting transfers between devices  39.6 us (28%)
  waiting for transfers between devices  38.6 us (27%)
  local copies, waits for them, and re-layouts  23.2 us (16%)
  Pallas kernels  22.9 us (16%)
  matrix products  8.87 us (6%)
  other arithmetic  4.97 us (4%)
    ppermute x3, waiting for transfers between devices, swap(): return lax.ppermute(slots, 'grp', swap_halves)  34.6 us
    all_to_all x3, starting transfers between devices, in_half(): lax.all_to_all(slots, 'grp', 0, 0, axis_index_groups=half_groups, tiled=T...  23.7 us
    ppermute x3, starting transfers between devices, swap(): return lax.ppermute(slots, 'grp', swap_halves)  12.5 us
    pallas_call x1, Pallas kernels, place_early(): pl.pallas_call(place_early_kernel, out_shape=jax.ShapeDtypeStruct((source...  6.33 us
    gather x1, local copies, waits for them, and re-layouts, attend_all(): cache[table, 1].reshape(request_list, section_span, kv_heads, HEAD_SIZE)  5.58 us
    gather x1, local copies, waits for them, and re-layouts, attend_all(): cache[table, 0].reshape(request_list, section_span, kv_heads, HEAD_SIZE)  5.56 us
    dot_general x1, matrix products, local(): jnp.einsum('rsk,kd->rsd', stacked, out_weight, preferred_element_type=jnp...  4.09 us
    pallas_call x1, Pallas kernels, pack(): pl.pallas_call(pack_kernel, out_shape=(jax.ShapeDtypeStruct((plane, steps...  4 us
  transfers between devices with their start and end apart: 10, of which 4 were waited for; matrix products, arithmetic and copies ran while one was open for 24% of the time, Pallas kernels for 12%

profile of v1, /device:TPU:12, one launch (start us, length us, event | category | flops | bytes accessed | tf_op | source)
XLA Modules:
  0.0 140.0 jit_solution(300359678678285381)
XLA Ops:
  0.7 0.8 select_reduce_fusion.1
  1.6 3.9 %first_pages.3 = (bf16[8,2,256,128]{3,2,1,0:T(8,128)(2,1)}, s32[33]{0:T(128)}) custom-call(s32[1]{0:T(128)} %bitcast.33.me_ref, s32[32]{0:T(128)S(1)} %get-tuple-element.160.own_ref, s32[32]{0:T(128)S(1)} %get-tuple-element.161.cross_ref, s32[32]{0:T(128)S(1)} %get-tuple-element.162.count_ref, s32[4,24]{1,0:T(4,128)} %bitcast.148, s32[1,16]{1,0:T(1,128)} %victim_ref.3, ...), custom_call_target="tpu_custom_call" | custom-call | tf_op jit(solution)/shard_map/first_pages/pallas_call | solution.py:162
  5.4 7.2 %collective-permute-start.7 = (bf16[8,2,256,128]{3,2,1,0:T(8,128)(2,1)}, bf16[8,2,256,128]{3,2,1,0:T(8,128)(2,1)}, u32[]{:S(2)}, u32[]{:S(2)}) collective-permute-start(bf16[8,2,256,128]{3,2,1,0:T(8,128)(2,1)} %get-tuple-element.86._), channel_id=1, source_target_pairs={{0,128},{8,136},{16,144},{24,152},{32,160},{40,168},{48,176},{56,1... | collective-permute-start | bytes 3145736 | tf_op jit(solution)/shard_map/ppermute | solution.py:486
  12.7 4.0 %pack_pages.3 = (bf16[16,3,256,128]{3,2,1,0:T(8,128)(2,1)}, bf16[8,256,128]{2,1,0:T(8,128)(2,1)}) custom-call(s32[1]{0:T(128)} %bitcast.33.me_ref, s32[33]{0:T(128)} %get-tuple-element.85.via_ref, s32[1,24]{1,0:T(1,128)S(1)} %copy-done.12, s32[4,24]{1,0:T(4,128)S(1)} %bitcast.149, s32[1,16]{1,0:T(1,128)S(1)} %copy-done.10, s32[16,32]{1,0:T(8,128)S(1)} %bitcast.137, ...), custom_call_target="tpu_custom_call" | custom-call | tf_op jit(solution)/shard_map/pack_pages/pallas_call | solution.py:257
  16.7 7.6 %all-to-all-start.3 = ((bf16[16,3,256,128]{3,2,1,0:T(8,128)(2,1)}), bf16[16,3,256,128]{3,2,1,0:T(8,128)(2,1)S(1)}, u32[]{:S(2)}, u32[]{:S(2)}) async-start(bf16[16,3,256,128]{3,2,1,0:T(8,128)(2,1)} %get-tuple-element.89), calls=%async_computation.3 | async-start | bytes 6291456 | tf_op jit(solution)/shard_map/all_to_all | solution.py:483
  24.7 5.6 %gather_fusion.1 = bf16[96,128,128]{2,1,0:T(8,128)(2,1)} fusion(bf16[80,2,128,128]{3,2,1,0:T(8,128)(2,1)} %bitcast.132, s32[96]{0:T(128)S(1)} %reshape.187), kind=kCustom, calls=%fused_computation.1 | custom fusion | bytes 6292224 | tf_op jit(solution)/shard_map/gather | solution.py:23
  30.3 5.6 %gather_fusion = bf16[96,128,128]{2,1,0:T(8,128)(2,1)} fusion(bf16[80,2,128,128]{3,2,1,0:T(8,128)(2,1)} %bitcast.133, s32[96]{0:T(128)S(1)} %reshape.181), kind=kCustom, calls=%fused_computation | custom fusion | bytes 6292224 | tf_op jit(solution)/shard_map/gather | solution.py:24
  36.5 3.2 %fusion.39 = (f32[24,4,3]{1,2,0:T(4,128)S(1)}, f32[24,1,4,3,512]{4,2,3,0,1:T(4,128)S(1)}) fusion(bf16[24,512,128,1]{2,1,3,0:T(8,128)(2,1)} %bitcast.142, bf16[3,24,4,128]{3,2,1,0:T(4,128)(2,1)S(1)} %reshape.171, pred[24,512]{1,0:T(8,128)(4,1)S(1)} %iota_compare_fusion), kind=kOutput, calls=%fused_computation.76 | convolution fusion | flops 38190816 | bytes 3822720 | tf_op jit(solution)/shard_map/srhgd,rkhd->rhgsk/dot_general | solution.py:32
  41.5 4.1 %fusion = f32[24,3,4096]{2,0,1:T(8,128)} fusion(bf16[512,4096]{1,0:T(8,128)(2,1)} %param.14, bf16[3,24,512]{2,1,0:T(8,128)(2,1)S(1)} %reshape.176), kind=kOutput, calls=%fused_computation.2 | convolution fusion | flops 301989888 | bytes 5447680 | tf_op jit(solution)/shard_map/rsk,kd->rsd/dot_general | solution.py:505
  45.5 2.6 %reshape.177 = f32[4,2,3,3,4096]{4,2,1,0,3:T(4,128)} reshape(f32[24,3,4096]{2,0,1:T(8,128)} %fusion) | data formatting | bytes 2359296 | tf_op jit(solution)/shard_map/reshape | solution.py:506
  48.2 2.5 %constant_dynamic-slice_fusion.5 = (f32[4,1,3,3,4096]{4,2,1,0,3:T(4,128)}, f32[4,1,3,3,4096]{4,2,1,0,3:T(4,128)S(1)}) fusion(f32[4,2,3,3,4096]{4,2,1,0,3:T(4,128)} %reshape.177, s32[]{:T(128)S(6)} %select_n.103, s32[]{:T(128)S(6)} %select_n.104), kind=kLoop, calls=%fused_computation.69 | loop fusion | bytes 2359304 | tf_op jit(solution)/shard_map/jit(dynamic_index_in_dim)/dynamic_slice | solution.py:507
  50.7 1.2 copy.79
  51.9 5.5 %collective-permute-done.7.got_ref = bf16[8,2,256,128]{3,2,1,0:T(8,128)(2,1)} collective-permute-done((bf16[8,2,256,128]{3,2,1,0:T(8,128)(2,1)}, bf16[8,2,256,128]{3,2,1,0:T(8,128)(2,1)}, u32[]{:S(2)}, u32[]{:S(2)}) %collective-permute-start.7) | collective-permute-done | bytes 1048608 | tf_op jit(solution)/shard_map/ppermute | solution.py:486
  57.4 2.1 %relay_pages.7 = bf16[16,2,256,128]{3,2,1,0:T(8,128)(2,1)} custom-call(s32[1]{0:T(128)} %bitcast.33.me_ref, s32[33]{0:T(128)} %get-tuple-element.85.via_ref, s32[16,32]{1,0:T(8,128)S(1)} %bitcast.138, bf16[8,2,256,128]{3,2,1,0:T(8,128)(2,1)} %collective-permute-done.7.got_ref), custom_call_target="tpu_custom_call" | custom-call | tf_op jit(solution)/shard_map/relay_pages/pallas_call | solution.py:304
  59.6 4.0 %all-to-all-done.3.own_ref = bf16[16,3,256,128]{3,2,1,0:T(8,128)(2,1)S(1)} async-done(((bf16[16,3,256,128]{3,2,1,0:T(8,128)(2,1)}), bf16[16,3,256,128]{3,2,1,0:T(8,128)(2,1)S(1)}, u32[]{:S(2)}, u32[]{:S(2)}) %all-to-all-start.3) | async-done | bytes 3145760 | tf_op jit(solution)/shard_map/all_to_all | solution.py:483
  63.5 8.8 %all-to-all-start.4 = ((bf16[16,2,256,128]{3,2,1,0:T(8,128)(2,1)}), bf16[16,2,256,128]{3,2,1,0:T(8,128)(2,1)}, u32[]{:S(2)}, u32[]{:S(2)}) async-start(bf16[16,2,256,128]{3,2,1,0:T(8,128)(2,1)} %relay_pages.7), calls=%async_computation.4 | async-start | bytes 4194304 | tf_op jit(solution)/shard_map/all_to_all | solution.py:483
  72.4 2.6 %fusion.37 = (bf16[4,3,3,4096]{3,0,2,1:T(4,128)(2,1)S(1)}, f32[4,3,3,4096]{3,0,2,1:T(4,128)}) fusion(f32[4,3,3,4096]{3,0,2,1:T(4,128)} %collective-permute-done.2, f32[4,1,3,3,4096]{4,2,1,0,3:T(4,128)} %get-tuple-element.130), kind=kLoop, calls=%fused_computation.74 | loop fusion | flops 294912 | bytes 2064384 | tf_op jit(solution)/shard_map/convert_element_type | solution.py:511
  75.0 2.2 %collective-permute-start.6 = (bf16[8,256,128]{2,1,0:T(8,128)(2,1)}, bf16[8,256,128]{2,1,0:T(8,128)(2,1)S(1)}, u32[]{:S(2)}, u32[]{:S(2)}) collective-permute-start(bf16[8,256,128]{2,1,0:T(8,128)(2,1)} %get-tuple-element.88), channel_id=1, source_target_pairs={{0,128},{8,136},{16,144},{24,152},{32,160},{40,168},{48,176},{56,1... | collective-permute-start | bytes 1572872 | tf_op jit(solution)/shard_map/ppermute | solution.py:486
  78.7 0.7 collective-permute-start.4
  79.4 2.8 %collective-permute-start.5 = (bf16[3,3,4096]{2,1,0:T(4,128)(2,1)S(1)}, bf16[3,3,4096]{2,1,0:T(4,128)(2,1)S(1)}, u32[]{:S(2)}, u32[]{:S(2)}) collective-permute-start(bf16[3,3,4096]{2,1,0:T(4,128)(2,1)S(1)} %bitcast.152), channel_id=1, source_target_pairs={{0,6},{1,7},{2,0},{3,1},{4,2},{5,3},{6,4},{7,5},{8,14},{9,15},{10,... | collective-permute-start | bytes 221192 | tf_op jit(solution)/shard_map/ppermute | solution.py:514
  82.2 22.1 %collective-permute-done.6.got_ref = bf16[8,256,128]{2,1,0:T(8,128)(2,1)S(1)} collective-permute-done((bf16[8,256,128]{2,1,0:T(8,128)(2,1)}, bf16[8,256,128]{2,1,0:T(8,128)(2,1)S(1)}, u32[]{:S(2)}, u32[]{:S(2)}) %collective-permute-start.6) | collective-permute-done | bytes 524320 | tf_op jit(solution)/shard_map/ppermute | solution.py:486
  104.3 0.8 copy-done.8
  105.1 1.9 %relay_pages.6 = bf16[16,256,128]{2,1,0:T(8,128)(2,1)} custom-call(s32[1]{0:T(128)} %bitcast.33.me_ref, s32[33]{0:T(128)} %get-tuple-element.85.via_ref, s32[16,32]{1,0:T(8,128)S(1)} %bitcast.139, bf16[8,256,128]{2,1,0:T(8,128)(2,1)} %copy-done.8), custom_call_target="tpu_custom_call" | custom-call | tf_op jit(solution)/shard_map/relay_pages/pallas_call | solution.py:304
  107.0 2.1 %lift_pages.1 = bf16[2,3,256,128]{3,2,1,0:T(8,128)(2,1)} custom-call(s32[1]{0:T(128)} %bitcast.33.me_ref, s32[33]{0:T(128)} %get-tuple-element.85.via_ref, bf16[16,3,256,128]{3,2,1,0:T(8,128)(2,1)} %copy-done.3), custom_call_target="tpu_custom_call" | custom-call | tf_op jit(solution)/shard_map/lift_pages/pallas_call | solution.py:338
  109.1 7.3 %all-to-all-start.5 = ((bf16[16,256,128]{2,1,0:T(8,128)(2,1)}), bf16[16,256,128]{2,1,0:T(8,128)(2,1)}, u32[]{:S(2)}, u32[]{:S(2)}) async-start(bf16[16,256,128]{2,1,0:T(8,128)(2,1)} %relay_pages.6), calls=%async_computation.5 | async-start | bytes 2097152 | tf_op jit(solution)/shard_map/all_to_all | solution.py:483
  116.3 1.2 constant_dynamic-slice_fusion.3
  117.6 3.1 %collective-permute-start.8 = (bf16[2,3,256,128]{3,2,1,0:T(8,128)(2,1)}, bf16[2,3,256,128]{3,2,1,0:T(8,128)(2,1)}, u32[]{:S(2)}, u32[]{:S(2)}) collective-permute-start(bf16[2,3,256,128]{3,2,1,0:T(8,128)(2,1)} %lift_pages.1), channel_id=1, source_target_pairs={{0,128},{8,136},{16,144},{24,152},{32,160},{40,168},{48,176},{56,1... | collective-permute-start | bytes 1179656 | tf_op jit(solution)/shard_map/ppermute | solution.py:486
  120.7 0.8 fusion.20
  121.5 6.3 %place_early.3._ = bf16[16,3,256,128]{3,2,1,0:T(8,128)(2,1)S(1)} custom-call(s32[1]{0:T(128)} %bitcast.33.me_ref, s32[33]{0:T(128)} %get-tuple-element.85.via_ref, s32[16]{0:T(128)S(1)} %get-tuple-element.170.source_ref, bf16[16,3,256,128]{3,2,1,0:T(8,128)(2,1)} %copy-done.3, bf16[16,2,256,128]{3,2,1,0:T(8,128)(2,1)} %all-to-all-done.4.early_ref), custom_call_target="tpu_custom_call" | custom-call | tf_op jit(solution)/shard_map/place_early/pallas_call | solution.py:414
  127.8 7.0 %collective-permute-done.8.lifted_ref = bf16[2,3,256,128]{3,2,1,0:T(8,128)(2,1)} collective-permute-done((bf16[2,3,256,128]{3,2,1,0:T(8,128)(2,1)}, bf16[2,3,256,128]{3,2,1,0:T(8,128)(2,1)}, u32[]{:S(2)}, u32[]{:S(2)}) %collective-permute-start.8) | collective-permute-done | bytes 393248 | tf_op jit(solution)/shard_map/ppermute | solution.py:486
  134.8 2.7 %place_late.3 = bf16[16,3,256,128]{3,2,1,0:T(8,128)(2,1)S(1)} custom-call(s32[1]{0:T(128)} %bitcast.33.me_ref, s32[33]{0:T(128)} %get-tuple-element.85.via_ref, s32[16]{0:T(128)S(1)} %get-tuple-element.170.source_ref, bf16[16,256,128]{2,1,0:T(8,128)(2,1)} %all-to-all-done.5.late_ref, ...), custom_call_target="tpu_custom_call", output_to_operand_aliasing={{}: (5, {})} | custom-call | tf_op jit(solution)/shard_map/place_late/pallas_call | solution.py:428
  137.6 1.7 %copy-done.1 = bf16[16,3,256,128]{3,2,1,0:T(8,128)(2,1)} copy-done((bf16[16,3,256,128]{3,2,1,0:T(8,128)(2,1)}, bf16[16,3,256,128]{3,2,1,0:T(8,128)(2,1)S(1)}, u32[]{:S(2)}) %copy-start.1) | copy-done | bytes 3145752
  (55 shorter events, 4.9 us)
Async XLA Ops:
  0.6 12.0 %copy-start.4 = (s32[32,16]{0,1:T(8,128)S(1)}, s32[32,16]{0,1:T(8,128)}, u32[]{:S(2)}) copy-start(s32[32,16]{0,1:T(8,128)} %param.18) | copy-start | bytes 6148
  0.6 12.0 %copy-start.10 = (s32[1,16]{1,0:T(1,128)S(1)}, s32[1,16]{1,0:T(1,128)}, u32[]{:S(2)}) copy-start(s32[1,16]{1,0:T(1,128)} %victim_ref.3) | copy-start | bytes 196
  0.7 12.0 %copy-start.9 = (s32[1,24,4]{1,2,0:T(4,128)S(1)}, s32[1,24,4]{1,2,0:T(4,128)}, u32[]{:S(2)}) copy-start(s32[1,24,4]{1,2,0:T(4,128)} %param.16) | copy-start | bytes 1156
  0.7 11.9 %copy-start.12 = (s32[1,24]{1,0:T(1,128)S(1)}, s32[1,24]{1,0:T(1,128)}, u32[]{:S(2)}) copy-start(s32[1,24]{1,0:T(1,128)} %length_ref.1) | copy-start | bytes 292
  0.7 12.0 %copy-start.7 = (s32[32,16,3]{0,1,2:T(8,128)S(1)}, s32[32,16,3]{0,1,2:T(8,128)}, u32[]{:S(2)}) copy-start(s32[32,16,3]{0,1,2:T(8,128)} %param.19) | copy-start | bytes 18436
  0.7 12.0 %copy-start.6 = (bf16[3,1,24,2,128]{4,3,2,1,0:T(2,128)(2,1)S(1)}, bf16[3,1,24,2,128]{4,3,2,1,0:T(2,128)(2,1)}, u32[]{:S(2)}) copy-start(bf16[3,1,24,2,128]{4,3,2,1,0:T(2,128)(2,1)} %param.12) | copy-start | bytes 110596
  5.4 52.0 %collective-permute-start.7 = (bf16[8,2,256,128]{3,2,1,0:T(8,128)(2,1)}, bf16[8,2,256,128]{3,2,1,0:T(8,128)(2,1)}, u32[]{:S(2)}, u32[]{:S(2)}) collective-permute-start(bf16[8,2,256,128]{3,2,1,0:T(8,128)(2,1)} %get-tuple-element.86._), channel_id=1, source_target_pairs={{0,128},{8,136},{16,144},{24,152},{32,160},{40,168},{48,176},{56,1... | collective-permute-start | bytes 3145736 | tf_op jit(solution)/shard_map/ppermute | solution.py:486
  16.7 8.0 %copy-start.11 = (bf16[3,1,24,512]{3,2,1,0:T(8,128)(2,1)S(1)}, bf16[3,1,24,512]{3,2,1,0:T(8,128)(2,1)}, u32[]{:S(2)}) copy-start(bf16[3,1,24,512]{3,2,1,0:T(8,128)(2,1)} %param.11) | copy-start | bytes 221188
  16.7 46.8 %all-to-all-start.3 = ((bf16[16,3,256,128]{3,2,1,0:T(8,128)(2,1)}), bf16[16,3,256,128]{3,2,1,0:T(8,128)(2,1)S(1)}, u32[]{:S(2)}, u32[]{:S(2)}) async-start(bf16[16,3,256,128]{3,2,1,0:T(8,128)(2,1)} %get-tuple-element.89), calls=%async_computation.3 | async-start | bytes 6291456 | tf_op jit(solution)/shard_map/all_to_all | solution.py:483
  35.9 4.7 %copy-start.5 = (bf16[96,128,128]{2,1,0:T(8,128)(2,1)S(1)}, bf16[96,128,128]{2,1,0:T(8,128)(2,1)}, u32[]{:S(2)}) copy-start(bf16[96,128,128]{2,1,0:T(8,128)(2,1)} %gather_fusion) | copy-start | bytes 9437188
  51.9 20.4 %collective-permute-start.2 = (f32[4,3,3,4096]{3,0,2,1:T(4,128)}, f32[4,3,3,4096]{3,0,2,1:T(4,128)}, u32[]{:S(2)}, u32[]{:S(2)}) collective-permute-start(f32[4,3,3,4096]{3,0,2,1:T(4,128)} %bitcast.126), channel_id=1, source_target_pairs={{0,1},{1,0},{2,3},{3,2},{4,5},{5,4},{6,7},{7,6},{8,9},{9,8},{10,11... | collective-permute-start | bytes 1769480 | tf_op jit(solution)/shard_map/ppermute | solution.py:509
  59.5 17.7 %copy-start.13 = (s32[33]{0:T(128)S(1)}, s32[33]{0:T(128)}, u32[]{:S(2)}) copy-start(s32[33]{0:T(128)} %get-tuple-element.85.via_ref) | copy-start | bytes 400
  63.5 11.5 %copy-start.3 = (bf16[16,3,256,128]{3,2,1,0:T(8,128)(2,1)}, bf16[16,3,256,128]{3,2,1,0:T(8,128)(2,1)S(1)}, u32[]{:S(2)}) copy-start(bf16[16,3,256,128]{3,2,1,0:T(8,128)(2,1)S(1)} %all-to-all-done.3.own_ref) | copy-start | bytes 9437188
  63.5 45.5 %all-to-all-start.4 = ((bf16[16,2,256,128]{3,2,1,0:T(8,128)(2,1)}), bf16[16,2,256,128]{3,2,1,0:T(8,128)(2,1)}, u32[]{:S(2)}, u32[]{:S(2)}) async-start(bf16[16,2,256,128]{3,2,1,0:T(8,128)(2,1)} %relay_pages.7), calls=%async_computation.4 | async-start | bytes 4194304 | tf_op jit(solution)/shard_map/all_to_all | solution.py:483
  75.0 29.3 %collective-permute-start.6 = (bf16[8,256,128]{2,1,0:T(8,128)(2,1)}, bf16[8,256,128]{2,1,0:T(8,128)(2,1)S(1)}, u32[]{:S(2)}, u32[]{:S(2)}) collective-permute-start(bf16[8,256,128]{2,1,0:T(8,128)(2,1)} %get-tuple-element.88), channel_id=1, source_target_pairs={{0,128},{8,136},{16,144},{24,152},{32,160},{40,168},{48,176},{56,1... | collective-permute-start | bytes 1572872 | tf_op jit(solution)/shard_map/ppermute | solution.py:486
  78.7 42.0 %collective-permute-start.4 = (bf16[3,3,4096]{2,1,0:T(4,128)(2,1)S(1)}, bf16[3,3,4096]{2,1,0:T(4,128)(2,1)S(1)}, u32[]{:S(2)}, u32[]{:S(2)}) collective-permute-start(bf16[3,3,4096]{2,1,0:T(4,128)(2,1)S(1)} %bitcast.153), channel_id=1, source_target_pairs={{0,4},{1,5},{2,6},{3,7},{4,0},{5,1},{6,2},{7,3},{8,12},{9,13},{10,... | collective-permute-start | bytes 221192 | tf_op jit(solution)/shard_map/ppermute | solution.py:514
  79.4 41.3 %collective-permute-start.5 = (bf16[3,3,4096]{2,1,0:T(4,128)(2,1)S(1)}, bf16[3,3,4096]{2,1,0:T(4,128)(2,1)S(1)}, u32[]{:S(2)}, u32[]{:S(2)}) collective-permute-start(bf16[3,3,4096]{2,1,0:T(4,128)(2,1)S(1)} %bitcast.152), channel_id=1, source_target_pairs={{0,6},{1,7},{2,0},{3,1},{4,2},{5,3},{6,4},{7,5},{8,14},{9,15},{10,... | collective-permute-start | bytes 221192 | tf_op jit(solution)/shard_map/ppermute | solution.py:514
  82.2 38.5 %collective-permute-start.3 = (bf16[3,3,4096]{2,1,0:T(4,128)(2,1)S(1)}, bf16[3,3,4096]{2,1,0:T(4,128)(2,1)S(1)}, u32[]{:S(2)}, u32[]{:S(2)}) collective-permute-start(bf16[3,3,4096]{2,1,0:T(4,128)(2,1)S(1)} %bitcast.151), channel_id=1, source_target_pairs={{0,2},{1,3},{2,4},{3,5},{4,6},{5,7},{6,0},{7,1},{8,10},{9,11},{10,... | collective-permute-start | bytes 221192 | tf_op jit(solution)/shard_map/ppermute | solution.py:514
  104.3 0.8 copy-start.8
  109.1 25.8 %all-to-all-start.5 = ((bf16[16,256,128]{2,1,0:T(8,128)(2,1)}), bf16[16,256,128]{2,1,0:T(8,128)(2,1)}, u32[]{:S(2)}, u32[]{:S(2)}) async-start(bf16[16,256,128]{2,1,0:T(8,128)(2,1)} %relay_pages.6), calls=%async_computation.5 | async-start | bytes 2097152 | tf_op jit(solution)/shard_map/all_to_all | solution.py:483
  117.6 17.3 %collective-permute-start.8 = (bf16[2,3,256,128]{3,2,1,0:T(8,128)(2,1)}, bf16[2,3,256,128]{3,2,1,0:T(8,128)(2,1)}, u32[]{:S(2)}, u32[]{:S(2)}) collective-permute-start(bf16[2,3,256,128]{3,2,1,0:T(8,128)(2,1)} %lift_pages.1), channel_id=1, source_target_pairs={{0,128},{8,136},{16,144},{24,152},{32,160},{40,168},{48,176},{56,1... | collective-permute-start | bytes 1179656 | tf_op jit(solution)/shard_map/ppermute | solution.py:486
  137.5 1.7 %copy-start.1 = (bf16[16,3,256,128]{3,2,1,0:T(8,128)(2,1)}, bf16[16,3,256,128]{3,2,1,0:T(8,128)(2,1)S(1)}, u32[]{:S(2)}) copy-start(bf16[16,3,256,128]{3,2,1,0:T(8,128)(2,1)S(1)} %place_late.3) | copy-start | bytes 9437188

commit v2 on v1

--- a/solution.py
+++ b/solution.py
@@ -1,3 +1,4 @@
+import functools
 import math
 
 import jax
@@ -11,57 +12,138 @@
 HALVES = 2
 STRAIGHT = 8
 LIFTED = 2
+RELAY_FIRST = 20.3
+RELAY_LAST = 20
+PLACE_FIRST = 15
+ALL_VMEM = 62 * 2**20
+FREE = pl.CostEstimate(flops=0, bytes_accessed=0, transcendentals=0)
 
 
 masked_score = -1e30
 
 
-def attend_all(query_steps, fresh_steps, cache, table, request_lengths, kv_heads, query_heads):
-    steps_total, request_list = (query_steps.shape[0], query_steps.shape[1])
-    entries = table.shape[1]
-    section_span = entries * cache.shape[2]
-    key_rows = cache[table, 0].reshape(request_list, section_span, kv_heads, HEAD_SIZE)
-    value_rows = cache[table, 1].reshape(request_list, section_span, kv_heads, HEAD_SIZE)
-    grouped_heads = query_steps.reshape(
-        steps_total, request_list, kv_heads, query_heads // kv_heads, HEAD_SIZE
-    )
-    fresh_keys = fresh_steps[:, :, 0].reshape(steps_total, request_list, kv_heads, HEAD_SIZE)
-    fresh_values = fresh_steps[:, :, 1].reshape(steps_total, request_list, kv_heads, HEAD_SIZE)
-    scale = math.sqrt(HEAD_SIZE)
-    old_scores = (
-        jnp.einsum("srhgd,rkhd->rhgsk", grouped_heads, key_rows, preferred_element_type=jnp.float32)
-        / scale
-    )
-    new_scores = (
-        jnp.einsum(
-            "srhgd,trhd->rhgst", grouped_heads, fresh_keys, preferred_element_type=jnp.float32
+def attend_kernel(
+    per_rank,
+    core_ref,
+    length_ref,
+    table_ref,
+    query_ref,
+    fresh_ref,
+    cache_ref,
+    weight_ref,
+    _,
+    kept_ref,
+    given_ref,
+    pool,
+    weight,
+    attended,
+    sems,
+):
+    entries, requests = table_ref.shape
+    steps = fresh_ref.shape[2]
+    page_len = cache_ref.shape[1] // 2
+    padded = query_ref.shape[1]
+    heads = attended.shape[2] // HEAD_SIZE
+    pool_in = pltpu.make_async_copy(cache_ref, pool, sems.at[0])
+    weight_in = pltpu.make_async_copy(weight_ref, weight, sems.at[1])
+    pool_in.start()
+    weight_in.start()
+    attended[...] = jnp.zeros_like(attended)
+    pool_in.wait()
+    tile = 16
+    tile_rows = lax.broadcasted_iota(jnp.int32, (tile, HEAD_SIZE), 0)
+    columns = lax.broadcasted_iota(jnp.int32, (padded, entries * page_len), 1)
+    row_steps = lax.broadcasted_iota(jnp.int32, (padded, entries * page_len), 0) // heads
+    scale = 1.0 / math.sqrt(HEAD_SIZE)
+    for r in range(requests):
+        length = length_ref[0, r]
+        for t in range(steps):
+            position = length + t
+            page = table_ref[position // page_len, r]
+            row = position % page_len
+            base = (row // tile) * tile
+            for side in range(2):
+                span = pl.ds(pl.multiple_of(side * page_len + base, tile), tile)
+                token = fresh_ref[r, side].astype(jnp.float32)[t : t + 1]
+                content = pool[page, span, :].astype(jnp.float32)
+                content = jnp.where(tile_rows == row - base, token, content)
+                pool[page, span, :] = content.astype(jnp.bfloat16)
+    for r in range(requests):
+        length = length_ref[0, r]
+        query = query_ref[r]
+        scores = jnp.concatenate(
+            [
+                lax.dot_general(
+                    query,
+                    pool[table_ref[p, r], pl.ds(0, page_len), :],
+                    (((1,), (1,)), ((), ())),
+                    preferred_element_type=jnp.float32,
+                )
+                for p in range(entries)
+            ],
+            axis=1,
         )
-        / scale
-    )
-    old_visible = jnp.arange(section_span)[None, :] < request_lengths[:, None]
-    old_scores = jnp.where(old_visible[:, None, None, None, :], old_scores, masked_score)
-    new_visible = jnp.arange(steps_total)[None, :] <= jnp.arange(steps_total)[:, None]
-    new_scores = jnp.where(new_visible[None, None, None, :, :], new_scores, masked_score)
-    peak = jnp.maximum(
-        jnp.max(old_scores, axis=-1, keepdims=True), jnp.max(new_scores, axis=-1, keepdims=True)
-    )
-    old_weights = jnp.exp(old_scores - peak)
-    new_weights = jnp.exp(new_scores - peak)
-    total = jnp.sum(old_weights, axis=-1) + jnp.sum(new_weights, axis=-1)
-    old_probs = old_weights.astype(jnp.bfloat16)
-    new_probs = new_weights.astype(jnp.bfloat16)
-    summed = jnp.einsum(
-        "rhgsk,rkhd->srhgd", old_probs, value_rows, preferred_element_type=jnp.float32
-    )
-    summed = summed + jnp.einsum(
-        "rhgst,trhd->srhgd", new_probs, fresh_values, preferred_element_type=jnp.float32
-    )
-    total = jnp.moveaxis(total, 3, 0)[..., None]
-    return (
-        (summed / total)
-        .astype(jnp.bfloat16)
-        .reshape(steps_total, request_list, query_heads * HEAD_SIZE)
-    )
+        scores = jnp.where(columns <= length + row_steps, scores * scale, masked_score)
+        weights = jnp.exp(scores - jnp.max(scores, axis=1, keepdims=True))
+        total = jnp.sum(weights, axis=1, keepdims=True)
+        probs = weights.astype(jnp.bfloat16)
+        summed = jnp.zeros((padded, HEAD_SIZE), jnp.float32)
+        for p in range(entries):
+            summed = summed + jnp.dot(
+                probs[:, p * page_len : (p + 1) * page_len],
+                pool[table_ref[p, r], pl.ds(page_len, page_len), :],
+                preferred_element_type=jnp.float32,
+            )
+        result = (summed / total).astype(jnp.bfloat16).astype(jnp.float32)
+        block, place = divmod(r, per_rank)
+        side = (block % 2) ^ core_ref[0]
+        for t in range(steps):
+            row = ((block // 2) * per_rank + place) * steps + t
+            for h in range(heads):
+                attended[side, row, pl.ds(h * HEAD_SIZE, HEAD_SIZE)] = result[t * heads + h]
+    weight_in.wait()
+    rows = kept_ref.shape[0]
+    left = attended[...].astype(jnp.bfloat16)
+    width = 512
+
+    def project(n, carry):
+        span = pl.ds(pl.multiple_of(n * width, width), width)
+        for side, out_ref in enumerate((kept_ref, given_ref)):
+            product = jnp.dot(left[side], weight[:, span], preferred_element_type=jnp.float32)
+            out_ref[:, span] = product[:rows]
+        return carry
+
+    lax.fori_loop(0, weight.shape[1] // width, project, 0)
+
+
+def attend(core, lengths, table, queries, fresh, cache, out_weight, ranks, after):
+    steps, requests, features = queries.shape
+    heads = features // HEAD_SIZE
+    by_request = queries.reshape(steps, requests, heads, HEAD_SIZE).transpose(1, 0, 2, 3)
+    by_request = by_request.reshape(requests, steps * heads, HEAD_SIZE)
+    by_request = jnp.pad(by_request, ((0, 0), (0, -(steps * heads) % 16), (0, 0)))
+    fresh = fresh.transpose(1, 2, 0, 3)
+    rows = requests * steps // 2
+    padded = rows + (-rows) % 8
+    smem = pl.BlockSpec(memory_space=pltpu.SMEM)
+    vmem = pl.BlockSpec(memory_space=pltpu.VMEM)
+    anywhere = pl.BlockSpec(memory_space=pl.ANY)
+    half = jax.ShapeDtypeStruct((rows, out_weight.shape[1]), jnp.float32)
+    return pl.pallas_call(
+        functools.partial(attend_kernel, requests // ranks),
+        out_shape=(half, half),
+        in_specs=[smem, smem, smem, vmem, vmem, anywhere, anywhere, anywhere],
+        out_specs=(vmem, vmem),
+        scratch_shapes=[
+            pltpu.VMEM(cache.shape, cache.dtype),
+            pltpu.VMEM(out_weight.shape, out_weight.dtype),
+            pltpu.VMEM((2, padded, features), jnp.float32),
+            pltpu.SemaphoreType.DMA((2,)),
+        ],
+        compiler_params=pltpu.CompilerParams(vmem_limit_bytes=40 * 2**20),
+        cost_estimate=FREE,
+        name="attend_and_project",
+    )(core, lengths, table, by_request, fresh, cache, out_weight, after)
 
 
 def route(own_ref, cross_ref, count_ref, via_ref, half, plane, straight):
@@ -172,6 +254,7 @@
             pltpu.SemaphoreType.DMA((count,)),
             pltpu.SemaphoreType.DMA,
         ],
+        cost_estimate=FREE,
         name="first_pages",
     )(me, *masks, table, victims, dest, cache)
 
@@ -267,6 +350,7 @@
             pltpu.SemaphoreType.DMA((count,)),
             pltpu.SemaphoreType.DMA,
         ],
+        cost_estimate=FREE,
         name="pack_pages",
     )(*scalars, fresh, cache, early)
 
@@ -299,7 +383,11 @@
     visit(lambda copy: copy.wait())
 
 
-def relay(me, via, dest, got, plane):
+def cost(microseconds):
+    return pl.CostEstimate(flops=int(microseconds * 10**9), bytes_accessed=0, transcendentals=0)
+
+
+def relay(me, via, dest, got, plane, guess):
     smem = pl.BlockSpec(memory_space=pltpu.SMEM)
     return pl.pallas_call(
         relay_kernel,
@@ -307,6 +395,7 @@
         in_specs=[smem, smem, smem, pl.BlockSpec(memory_space=pltpu.VMEM)],
         out_specs=pl.BlockSpec(memory_space=pl.ANY),
         scratch_shapes=[pltpu.SemaphoreType.DMA],
+        cost_estimate=cost(guess),
         name="relay_pages",
     )(me, via, dest, got)
 
@@ -341,43 +430,15 @@
         in_specs=[smem, smem, pl.BlockSpec(memory_space=pltpu.VMEM)],
         out_specs=pl.BlockSpec(memory_space=pl.ANY),
         scratch_shapes=[pltpu.SemaphoreType.DMA],
+        cost_estimate=FREE,
         name="lift_pages",
     )(me, via, own)
 
 
-def place_early_kernel(me_ref, via_ref, source_ref, own_ref, early_ref, out_ref, sem):
+def place_first_kernel(
+    me_ref, via_ref, source_ref, own_ref, early_ref, lifted_ref, out_ref, rank_ref, sem
+):
     plane = own_ref.shape[0]
-    count, pages = out_ref.shape[:2]
-    group = me_ref[0]
-    my_half = group // plane
-
-    def visit(act):
-        for j in range(count):
-            source = source_ref[j]
-            near = (source // plane) == my_half
-            far = jnp.logical_not(near | goes_via(via_ref, source, group % plane))
-            place = source % plane
-
-            @pl.when(near)
-            def _():
-                act(pltpu.make_async_copy(own_ref.at[place], out_ref.at[j], sem))
-
-            @pl.when(far)
-            def _():
-                act(
-                    pltpu.make_async_copy(
-                        early_ref.at[place], out_ref.at[j, pl.ds(0, pages - 1)], sem
-                    )
-                )
-
-    visit(lambda copy: copy.start())
-    visit(lambda copy: copy.wait())
-
-
-def place_late_kernel(
-    me_ref, via_ref, source_ref, late_ref, lifted_ref, _, out_ref, rank_ref, sem
-):
-    plane = late_ref.shape[0]
     room = lifted_ref.shape[0]
     count, pages = out_ref.shape[:2]
     group = me_ref[0]
@@ -392,48 +453,81 @@
         for j in range(count):
             source = source_ref[j]
             place = source % plane
-            cross = (source // plane) != my_half
-            lifted = cross & goes_via(via_ref, source, group % plane)
-            far = cross & jnp.logical_not(lifted)
+            near = (source // plane) == my_half
+            via = goes_via(via_ref, source, group % plane)
+            lifted = jnp.logical_not(near) & via
+            far = jnp.logical_not(near | via)
+
+            @pl.when(near)
+            def _():
+                act(pltpu.make_async_copy(own_ref.at[place], out_ref.at[j], sem))
+
+            @pl.when(far)
+            def _():
+                act(
+                    pltpu.make_async_copy(
+                        early_ref.at[place], out_ref.at[j, pl.ds(0, pages - 1)], sem
+                    )
+                )
+
+            @pl.when(lifted)
+            def _():
+                act(pltpu.make_async_copy(lifted_ref.at[rank_ref[place]], out_ref.at[j], sem))
+
+    visit(lambda copy: copy.start())
+    visit(lambda copy: copy.wait())
+
+
+def place_late_kernel(me_ref, via_ref, source_ref, late_ref, _, out_ref, sem):
+    plane = late_ref.shape[0]
+    count, pages = out_ref.shape[:2]
+    group = me_ref[0]
+    my_half = group // plane
+
+    def visit(act):
+        for j in range(count):
+            source = source_ref[j]
+            place = source % plane
+            near = (source // plane) == my_half
+            far = jnp.logical_not(near | goes_via(via_ref, source, group % plane))
 
             @pl.when(far)
             def _():
                 act(pltpu.make_async_copy(late_ref.at[place], out_ref.at[j, pages - 1], sem))
 
-            @pl.when(lifted)
-            def _():
-                act(pltpu.make_async_copy(lifted_ref.at[rank_ref[place]], out_ref.at[j], sem))
-
     visit(lambda copy: copy.start())
     visit(lambda copy: copy.wait())
 
 
-def place_early(me, via, sources, own, early):
+def place_first(me, via, sources, own, early, lifted):
     smem = pl.BlockSpec(memory_space=pltpu.SMEM)
     vmem = pl.BlockSpec(memory_space=pltpu.VMEM)
     return pl.pallas_call(
-        place_early_kernel,
+        place_first_kernel,
         out_shape=jax.ShapeDtypeStruct((sources.shape[0],) + own.shape[1:], own.dtype),
-        in_specs=[smem, smem, smem, vmem, vmem],
-        out_specs=pl.BlockSpec(memory_space=pl.ANY),
-        scratch_shapes=[pltpu.SemaphoreType.DMA],
-        name="place_early",
-    )(me, via, sources, own, early)
-
-
-def place_late(me, via, sources, late, lifted, out):
+        in_specs=[smem, smem, smem, vmem, vmem, vmem],
+        out_specs=pl.BlockSpec(memory_space=pltpu.HBM),
+        scratch_shapes=[pltpu.SMEM((own.shape[0],), jnp.int32), pltpu.SemaphoreType.DMA],
+        compiler_params=pltpu.CompilerParams(vmem_limit_bytes=ALL_VMEM),
+        cost_estimate=cost(PLACE_FIRST),
+        name="place_first",
+    )(me, via, sources, own, early, lifted)
+
+
+def place_late(me, via, sources, late, out):
     smem = pl.BlockSpec(memory_space=pltpu.SMEM)
-    vmem = pl.BlockSpec(memory_space=pltpu.VMEM)
-    anywhere = pl.BlockSpec(memory_space=pl.ANY)
+    hbm = pl.BlockSpec(memory_space=pltpu.HBM)
     return pl.pallas_call(
         place_late_kernel,
         out_shape=jax.ShapeDtypeStruct(out.shape, out.dtype),
-        in_specs=[smem, smem, smem, vmem, vmem, anywhere],
-        out_specs=anywhere,
-        scratch_shapes=[pltpu.SMEM((late.shape[0],), jnp.int32), pltpu.SemaphoreType.DMA],
-        input_output_aliases={5: 0},
+        in_specs=[smem, smem, smem, pl.BlockSpec(memory_space=pltpu.VMEM), hbm],
+        out_specs=hbm,
+        scratch_shapes=[pltpu.SemaphoreType.DMA],
+        input_output_aliases={4: 0},
+        compiler_params=pltpu.CompilerParams(vmem_limit_bytes=ALL_VMEM),
+        cost_estimate=FREE,
         name="place_late",
-    )(me, via, sources, late, lifted, out)
+    )(me, via, sources, late, out)
 
 
 def local(
@@ -449,8 +543,6 @@
 ):
     steps_total = queries.shape[0]
     pool_pages, _, page_len, pair_width = cache_pool.shape[1:]
-    kv_heads = pair_width // HEAD_SIZE
-    query_heads = queries.shape[3] // HEAD_SIZE
     victim_count = victims.shape[1]
     groups = lax.axis_size("grp")
     ranks = lax.axis_size("tp")
@@ -492,21 +584,21 @@
     early_got = swap(early)
     own, late = pack(STRAIGHT, pack_args(via), fresh_steps, pages, plane, early)
     own_got = in_half(own)
-    attended = attend_all(
+    kept, given = attend(
+        core.astype(jnp.int32)[None],
+        lengths,
+        table,
         queries[:, 0],
         fresh_steps,
-        cache_pool[0],
-        page_table[0],
-        lengths[0],
-        kv_heads,
-        query_heads,
+        pages,
+        out_weight,
+        ranks,
+        own,
     )
-    stacked = jnp.moveaxis(attended, 0, 1)
-    partial = jnp.einsum("rsk,kd->rsd", stacked, out_weight, preferred_element_type=jnp.float32)
-    by_core = partial.reshape((chips, 2, -1) + partial.shape[1:])
-    kept = lax.dynamic_index_in_dim(by_core, core, 1, keepdims=False)
-    given = lax.dynamic_index_in_dim(by_core, 1 - core, 1, keepdims=False)
     on_chip = kept + lax.ppermute(given, "tp", swap_cores)
+    on_chip = on_chip.reshape(chips, -1, steps_total, on_chip.shape[1])
+    late, on_chip = lax.optimization_barrier((late, on_chip))
+    late_got = swap(late)
     projected = lax.dynamic_index_in_dim(on_chip, chip, 0, keepdims=False)
     on_chip = on_chip.astype(jnp.bfloat16)
     for shift in range(1, chips):
@@ -517,19 +609,15 @@
         projected = projected + share.astype(jnp.float32)
     projected = projected.astype(jnp.bfloat16)
 
-    late, on_chip = lax.optimization_barrier((late, on_chip))
-    late_got = swap(late)
-    early_slots = relay(me, via, dest, early_got, plane)
-    early_slots, own_got = lax.optimization_barrier((early_slots, own_got))
+    early_slots = relay(me, via, dest, early_got, plane, RELAY_FIRST)
     early_arrived = in_half(early_slots)
     lifted = lift(me, via, own_got)
-    lifted, early_arrived = lax.optimization_barrier((lifted, early_arrived))
+    lifted, late_got, projected = lax.optimization_barrier((lifted, late_got, projected))
     lifted_got = swap(lifted)
-    migrated = place_early(me, via, sources, own_got, early_arrived)
-    late_slots = relay(me, via, dest, late_got, plane)
-    late_slots, early_arrived = lax.optimization_barrier((late_slots, early_arrived))
+    migrated = place_first(me, via, sources, own_got, early_arrived, lifted_got)
+    late_slots = relay(me, via, dest, late_got, plane, RELAY_LAST)
     late_arrived = in_half(late_slots)
-    migrated = place_late(me, via, sources, late_arrived, lifted_got, migrated)
+    migrated = place_late(me, via, sources, late_arrived, migrated)
 
     def straight_only(carry):
         no_via = jnp.zeros_like(via)
@@ -538,11 +626,11 @@
         )
         own, late = pack(victim_count, pack_args(no_via), fresh_steps, pages, plane, early)
         own_got = in_half(own)
-        early_arrived = in_half(relay(me, no_via, dest, swap(early), plane))
-        late_arrived = in_half(relay(me, no_via, dest, swap(late), plane))
-        out = place_early(me, no_via, sources, own_got, early_arrived)
+        early_arrived = in_half(relay(me, no_via, dest, swap(early), plane, 0))
+        late_arrived = in_half(relay(me, no_via, dest, swap(late), plane, 0))
         lifted = jnp.zeros((LIFTED,) + own.shape[1:], own.dtype)
-        return jnp.int32(0), place_late(me, no_via, sources, late_arrived, lifted, out)
+        out = place_first(me, no_via, sources, own_got, early_arrived, lifted)
+        return jnp.int32(0), place_late(me, no_via, sources, late_arrived, out)
 
     _, migrated = lax.while_loop(lambda c: c[0] > 0, straight_only, (via[groups], migrated))
     migrated = migrated.reshape(1, victim_count, steps_total, 2, page_len, pair_width)

time: 141 us -> 130 us (0.922)
  the two profiles are of different devices: /device:TPU:12 before, /device:TPU:64 now
where the time goes in v2:
time: 130 us; the launch traced here: 129 us
  waiting for transfers between devices  46.4 us (36%)
  starting transfers between devices  35 us (27%)
  Pallas kernels  34.6 us (27%)
  local copies, waits for them, and re-layouts  7.22 us (6%)
  other arithmetic  3.8 us (3%)
    all_to_all x3, starting transfers between devices, in_half(): lax.all_to_all(slots, 'grp', 0, 0, axis_index_groups=half_groups, tiled=T...  19.3 us
    ppermute x3, waiting for transfers between devices, swap(): return lax.ppermute(slots, 'grp', swap_halves)  17.9 us
    ppermute x3, waiting for transfers between devices, local(): lax.ppermute(share, 'tp', [(r, (r + 2 * shift) % ranks) for r in range(ra...  17.9 us
    pallas_call x1, Pallas kernels, attend(): pl.pallas_call(functools.partial(attend_kernel, requests // ranks), out_s...  14.4 us
    ppermute x3, starting transfers between devices, swap(): return lax.ppermute(slots, 'grp', swap_halves)  11.3 us
    all_to_all x3, waiting for transfers between devices, in_half(): lax.all_to_all(slots, 'grp', 0, 0, axis_index_groups=half_groups, tiled=T...  8.88 us
    unnamed x29, local copies, waits for them, and re-layouts  6.16 us
    ppermute x3, starting transfers between devices, local(): lax.ppermute(share, 'tp', [(r, (r + 2 * shift) % ranks) for r in range(ra...  4.36 us
  transfers between devices with their start and end apart: 10, of which 8 were waited for; matrix products, arithmetic and copies ran while one was open for 3% of the time, Pallas kernels for 22%

profile of v2, /device:TPU:64, one launch (start us, length us, event | category | flops | bytes accessed | tf_op | source)
XLA Modules:
  0.0 128.7 jit_solution(3463443193037727254)
XLA Ops:
  0.7 0.9 select_reduce_fusion.1
  1.6 3.8 %first_pages.3 = (bf16[8,2,256,128]{3,2,1,0:T(8,128)(2,1)}, s32[33]{0:T(128)}) custom-call(s32[1]{0:T(128)} %bitcast.me_ref, s32[32]{0:T(128)S(1)} %get-tuple-element.194.own_ref, s32[32]{0:T(128)S(1)} %get-tuple-element.195.cross_ref, s32[32]{0:T(128)S(1)} %get-tuple-element.196.count_ref, s32[4,24]{1,0:T(4,128)} %bitcast.58, s32[1,16]{1,0:T(1,128)} %victim_ref.3, ...), custom_call_target="tpu_custom_call" | custom-call | tf_op jit(solution)/shard_map/first_pages/pallas_call | solution.py:244
  5.4 5.5 %collective-permute-start.7 = (bf16[8,2,256,128]{3,2,1,0:T(8,128)(2,1)}, bf16[8,2,256,128]{3,2,1,0:T(8,128)(2,1)}, u32[]{:S(2)}, u32[]{:S(2)}) collective-permute-start(bf16[8,2,256,128]{3,2,1,0:T(8,128)(2,1)} %get-tuple-element.87._), channel_id=1, source_target_pairs={{0,128},{8,136},{16,144},{24,152},{32,160},{40,168},{48,176},{56,1... | collective-permute-start | bytes 3145736 | tf_op jit(solution)/shard_map/ppermute | solution.py:578
  11.2 3.9 %pack_pages.3 = (bf16[16,3,256,128]{3,2,1,0:T(8,128)(2,1)}, bf16[8,256,128]{2,1,0:T(8,128)(2,1)}) custom-call(s32[1]{0:T(128)} %bitcast.me_ref, s32[33]{0:T(128)} %get-tuple-element.86.via_ref, s32[1,24]{1,0:T(1,128)S(1)} %copy-done.13, s32[4,24]{1,0:T(4,128)S(1)} %bitcast.59, s32[1,16]{1,0:T(1,128)S(1)} %copy-done.10, s32[16,32]{1,0:T(8,128)S(1)} %bitcast.52, ...), custom_call_target="tpu_custom_call" | custom-call | tf_op jit(solution)/shard_map/pack_pages/pallas_call | solution.py:340
  15.1 7.4 %all-to-all-start.3 = ((bf16[16,3,256,128]{3,2,1,0:T(8,128)(2,1)}), bf16[16,3,256,128]{3,2,1,0:T(8,128)(2,1)}, u32[]{:S(2)}, u32[]{:S(2)}) async-start(bf16[16,3,256,128]{3,2,1,0:T(8,128)(2,1)} %get-tuple-element.88._), calls=%async_computation.3 | async-start | bytes 6291456 | tf_op jit(solution)/shard_map/all_to_all | solution.py:575
  22.5 2.2 %copy-done.1 = bf16[512,4096]{1,0:T(8,128)(2,1)S(1)} copy-done((bf16[512,4096]{1,0:T(8,128)(2,1)S(1)}, bf16[512,4096]{1,0:T(8,128)(2,1)}, u32[]{:S(2)}) %copy-start.1) | copy-done | bytes 4194328
  24.7 14.4 %attend_and_project.1 = (f32[36,4096]{1,0:T(8,128)S(1)}, f32[36,4096]{1,0:T(8,128)}) custom-call(s32[1]{0:T(128)} %bitcast.9.core_ref, s32[1,24]{1,0:T(1,128)S(1)} %copy-done.13, s32[4,24]{1,0:T(4,128)S(1)} %bitcast.60, bf16[24,16,128]{2,1,0:T(8,128)(2,1)S(1)} %pad.4.query_ref, bf16[24,2,3,128]{3,2,1,0:T(4,128)(2,1)S(1)} %bitcast.45, ...), custom_call_target="tpu_custom_call" | custom-call | tf_op jit(solution)/shard_map/attend_and_project/pallas_call | solution.py:132
  39.1 0.8 copy-done.2
  40.0 0.6 slice.3
  40.5 1.7 %collective-permute-done.2 = f32[36,4096]{1,0:T(8,128)S(1)} collective-permute-done((f32[36,4096]{1,0:T(8,128)}, f32[36,4096]{1,0:T(8,128)S(1)}, u32[]{:S(2)}, u32[]{:S(2)}) %collective-permute-start.2) | collective-permute-done | bytes 589856 | tf_op jit(solution)/shard_map/ppermute | solution.py:598
  42.3 1.2 add.65
  43.7 0.7 collective-permute-start.3
  45.2 3.8 %collective-permute-start.5 = (bf16[3,3,4096]{2,1,0:T(4,128)(2,1)S(1)}, bf16[3,3,4096]{2,1,0:T(4,128)(2,1)S(1)}, u32[]{:S(2)}, u32[]{:S(2)}) collective-permute-start(bf16[3,3,4096]{2,1,0:T(4,128)(2,1)S(1)} %get-tuple-element.174), channel_id=1, source_target_pairs={{0,4},{1,5},{2,6},{3,7},{4,0},{5,1},{6,2},{7,3},{8,12},{9,13},{10,... | collective-permute-start | bytes 221192 | tf_op jit(solution)/shard_map/ppermute | solution.py:606
  49.0 9.3 %collective-permute-done.7.got_ref = bf16[8,2,256,128]{3,2,1,0:T(8,128)(2,1)} collective-permute-done((bf16[8,2,256,128]{3,2,1,0:T(8,128)(2,1)}, bf16[8,2,256,128]{3,2,1,0:T(8,128)(2,1)}, u32[]{:S(2)}, u32[]{:S(2)}) %collective-permute-start.7) | collective-permute-done | bytes 1048608 | tf_op jit(solution)/shard_map/ppermute | solution.py:578
  58.4 2.3 %relay_pages.7 = bf16[16,2,256,128]{3,2,1,0:T(8,128)(2,1)} custom-call(s32[1]{0:T(128)} %bitcast.me_ref, s32[33]{0:T(128)} %get-tuple-element.86.via_ref, s32[16,32]{1,0:T(8,128)S(1)} %bitcast.53, bf16[8,2,256,128]{3,2,1,0:T(8,128)(2,1)} %collective-permute-done.7.got_ref), custom_call_target="tpu_custom_call" | custom-call | flops 20299999232 | tf_op jit(solution)/shard_map/relay_pages/pallas_call | solution.py:392
  60.7 4.8 %all-to-all-done.3.own_ref = bf16[16,3,256,128]{3,2,1,0:T(8,128)(2,1)} async-done(((bf16[16,3,256,128]{3,2,1,0:T(8,128)(2,1)}), bf16[16,3,256,128]{3,2,1,0:T(8,128)(2,1)}, u32[]{:S(2)}, u32[]{:S(2)}) %all-to-all-start.3) | async-done | bytes 3145760 | tf_op jit(solution)/shard_map/all_to_all | solution.py:575
  65.5 5.1 %all-to-all-start.5 = ((bf16[16,2,256,128]{3,2,1,0:T(8,128)(2,1)}), bf16[16,2,256,128]{3,2,1,0:T(8,128)(2,1)S(1)}, u32[]{:S(2)}, u32[]{:S(2)}) async-start(bf16[16,2,256,128]{3,2,1,0:T(8,128)(2,1)} %relay_pages.7), calls=%async_computation.5 | async-start | bytes 4194304 | tf_op jit(solution)/shard_map/all_to_all | solution.py:575
  70.6 10.9 %collective-permute-done.6 = bf16[3,3,4096]{2,1,0:T(4,128)(2,1)S(1)} collective-permute-done((bf16[3,3,4096]{2,1,0:T(4,128)(2,1)S(1)}, bf16[3,3,4096]{2,1,0:T(4,128)(2,1)S(1)}, u32[]{:S(2)}, u32[]{:S(2)}) %collective-permute-start.6) | collective-permute-done | bytes 73760 | tf_op jit(solution)/shard_map/ppermute | solution.py:606
  81.5 5.0 %collective-permute-done.5 = bf16[3,3,4096]{2,1,0:T(4,128)(2,1)S(1)} collective-permute-done((bf16[3,3,4096]{2,1,0:T(4,128)(2,1)S(1)}, bf16[3,3,4096]{2,1,0:T(4,128)(2,1)S(1)}, u32[]{:S(2)}, u32[]{:S(2)}) %collective-permute-start.5) | collective-permute-done | bytes 73760 | tf_op jit(solution)/shard_map/ppermute | solution.py:606
  86.5 2.0 %collective-permute-done.4 = bf16[3,3,4096]{2,1,0:T(4,128)(2,1)} collective-permute-done((bf16[3,3,4096]{2,1,0:T(4,128)(2,1)S(1)}, bf16[3,3,4096]{2,1,0:T(4,128)(2,1)}, u32[]{:S(2)}, u32[]{:S(2)}) %collective-permute-start.4) | collective-permute-done | bytes 73760 | tf_op jit(solution)/shard_map/ppermute | solution.py:606
  88.5 1.6 %fusion.2 = bf16[3,3,4096]{2,1,0:T(4,128)(2,1)} fusion(bf16[3,3,4096]{2,1,0:T(4,128)(2,1)S(1)} %collective-permute-done.6, bf16[3,3,4096]{2,1,0:T(4,128)(2,1)S(1)} %collective-permute-done.5, bf16[3,3,4096]{2,1,0:T(4,128)(2,1)} %collective-permute-done.4, f32[4,3,3,4096]{3,2,1,0:T(4,128)S(1)} %reshape.35, s32[]{:T(128)S(6)} %select_n.76), kind=kLoop, calls=%fused_computation.3 | loop fusion | flops 258048 | bytes 442372 | tf_op jit(solution)/shard_map/convert_element_type | solution.py:610
  90.1 2.1 %lift_pages.1 = bf16[2,3,256,128]{3,2,1,0:T(8,128)(2,1)} custom-call(s32[1]{0:T(128)} %bitcast.me_ref, s32[33]{0:T(128)} %get-tuple-element.86.via_ref, bf16[16,3,256,128]{3,2,1,0:T(8,128)(2,1)} %all-to-all-done.3.own_ref), custom_call_target="tpu_custom_call" | custom-call | tf_op jit(solution)/shard_map/lift_pages/pallas_call | solution.py:427
  92.2 5.0 %collective-permute-start.8 = (bf16[2,3,256,128]{3,2,1,0:T(8,128)(2,1)}, bf16[2,3,256,128]{3,2,1,0:T(8,128)(2,1)S(1)}, u32[]{:S(2)}, u32[]{:S(2)}) collective-permute-start(bf16[2,3,256,128]{3,2,1,0:T(8,128)(2,1)} %lift_pages.1), channel_id=1, source_target_pairs={{0,128},{8,136},{16,144},{24,152},{32,160},{40,168},{48,176},{56,1... | collective-permute-start | bytes 1179656 | tf_op jit(solution)/shard_map/ppermute | solution.py:578
  97.2 2.0 %relay_pages.6 = bf16[16,256,128]{2,1,0:T(8,128)(2,1)} custom-call(s32[1]{0:T(128)} %bitcast.me_ref, s32[33]{0:T(128)} %get-tuple-element.86.via_ref, s32[16,32]{1,0:T(8,128)S(1)} %bitcast.54, bf16[8,256,128]{2,1,0:T(8,128)(2,1)} %collective-permute-done.3.got_ref), custom_call_target="tpu_custom_call" | custom-call | flops 20000000000 | tf_op jit(solution)/shard_map/relay_pages/pallas_call | solution.py:392
  99.2 1.3 %copy-done.7 = bf16[16,2,256,128]{3,2,1,0:T(8,128)(2,1)} copy-done((bf16[16,2,256,128]{3,2,1,0:T(8,128)(2,1)}, bf16[16,2,256,128]{3,2,1,0:T(8,128)(2,1)S(1)}, u32[]{:S(2)}) %copy-start.7) | copy-done | bytes 2097176
  100.5 6.9 %all-to-all-start.4 = ((bf16[16,256,128]{2,1,0:T(8,128)(2,1)}), bf16[16,256,128]{2,1,0:T(8,128)(2,1)S(1)}, u32[]{:S(2)}, u32[]{:S(2)}) async-start(bf16[16,256,128]{2,1,0:T(8,128)(2,1)} %relay_pages.6), calls=%async_computation.4 | async-start | bytes 2097152 | tf_op jit(solution)/shard_map/all_to_all | solution.py:575
  107.4 8.6 %collective-permute-done.8.lifted_ref = bf16[2,3,256,128]{3,2,1,0:T(8,128)(2,1)S(1)} collective-permute-done((bf16[2,3,256,128]{3,2,1,0:T(8,128)(2,1)}, bf16[2,3,256,128]{3,2,1,0:T(8,128)(2,1)S(1)}, u32[]{:S(2)}, u32[]{:S(2)}) %collective-permute-start.8) | collective-permute-done | bytes 393248 | tf_op jit(solution)/shard_map/ppermute | solution.py:578
  116.0 0.8 copy-done.15
  116.8 4.1 %place_first.3._ = bf16[16,3,256,128]{3,2,1,0:T(8,128)(2,1)} custom-call(s32[1]{0:T(128)} %bitcast.me_ref, s32[33]{0:T(128)} %get-tuple-element.86.via_ref, s32[16]{0:T(128)S(1)} %get-tuple-element.204.source_ref, bf16[16,3,256,128]{3,2,1,0:T(8,128)(2,1)} %all-to-all-done.3.own_ref, bf16[16,2,256,128]{3,2,1,0:T(8,128)(2,1)} %copy-done.7, ...), custom_call_target="tpu_custom_call" | custom-call | flops 15000000512 | tf_op jit(solution)/shard_map/place_first/pallas_call | solution.py:505
  120.9 4.1 %all-to-all-done.4.late_ref = bf16[16,256,128]{2,1,0:T(8,128)(2,1)S(1)} async-done(((bf16[16,256,128]{2,1,0:T(8,128)(2,1)}), bf16[16,256,128]{2,1,0:T(8,128)(2,1)S(1)}, u32[]{:S(2)}, u32[]{:S(2)}) %all-to-all-start.4) | async-done | bytes 1048608 | tf_op jit(solution)/shard_map/all_to_all | solution.py:575
  125.0 1.0 copy-done.6
  126.0 2.0 %place_late.3 = bf16[16,3,256,128]{3,2,1,0:T(8,128)(2,1)} custom-call(s32[1]{0:T(128)} %bitcast.me_ref, s32[33]{0:T(128)} %get-tuple-element.86.via_ref, s32[16]{0:T(128)S(1)} %get-tuple-element.204.source_ref, bf16[16,256,128]{2,1,0:T(8,128)(2,1)} %copy-done.6, bf16[16,3,256,128]{3,2,1,0:T(8,128)(2,1)} %place_first.3._), custom_call_target="tpu_custom_call", output_to_operand_aliasing={{}: (4, {})} | custom-call | tf_op jit(solution)/shard_map/place_late/pallas_call | solution.py:520
  (39 shorter events, 1.8 us)
Async XLA Ops:
  0.6 10.5 %copy-start.5 = (s32[32,16]{0,1:T(8,128)S(1)}, s32[32,16]{0,1:T(8,128)}, u32[]{:S(2)}) copy-start(s32[32,16]{0,1:T(8,128)} %param.18) | copy-start | bytes 6148
  0.6 10.5 %copy-start.9 = (s32[1,24,4]{1,2,0:T(4,128)S(1)}, s32[1,24,4]{1,2,0:T(4,128)}, u32[]{:S(2)}) copy-start(s32[1,24,4]{1,2,0:T(4,128)} %param.16) | copy-start | bytes 1156
  0.7 10.5 %copy-start.10 = (s32[1,16]{1,0:T(1,128)S(1)}, s32[1,16]{1,0:T(1,128)}, u32[]{:S(2)}) copy-start(s32[1,16]{1,0:T(1,128)} %victim_ref.3) | copy-start | bytes 196
  0.7 10.3 %copy-start.12 = (bf16[3,1,24,2,128]{4,3,2,1,0:T(2,128)(2,1)S(1)}, bf16[3,1,24,2,128]{4,3,2,1,0:T(2,128)(2,1)}, u32[]{:S(2)}) copy-start(bf16[3,1,24,2,128]{4,3,2,1,0:T(2,128)(2,1)} %param.12) | copy-start | bytes 110596
  0.7 10.4 %copy-start.11 = (bf16[3,1,24,512]{3,2,1,0:T(8,128)(2,1)S(1)}, bf16[3,1,24,512]{3,2,1,0:T(8,128)(2,1)}, u32[]{:S(2)}) copy-start(bf16[3,1,24,512]{3,2,1,0:T(8,128)(2,1)} %param.11) | copy-start | bytes 221188
  0.7 10.5 %copy-start.13 = (s32[1,24]{1,0:T(1,128)S(1)}, s32[1,24]{1,0:T(1,128)}, u32[]{:S(2)}) copy-start(s32[1,24]{1,0:T(1,128)} %length_ref.3) | copy-start | bytes 292
  0.7 10.5 %copy-start.8 = (s32[32,16,3]{0,1,2:T(8,128)S(1)}, s32[32,16,3]{0,1,2:T(8,128)}, u32[]{:S(2)}) copy-start(s32[32,16,3]{0,1,2:T(8,128)} %param.19) | copy-start | bytes 18436
  5.4 52.9 %collective-permute-start.7 = (bf16[8,2,256,128]{3,2,1,0:T(8,128)(2,1)}, bf16[8,2,256,128]{3,2,1,0:T(8,128)(2,1)}, u32[]{:S(2)}, u32[]{:S(2)}) collective-permute-start(bf16[8,2,256,128]{3,2,1,0:T(8,128)(2,1)} %get-tuple-element.87._), channel_id=1, source_target_pairs={{0,128},{8,136},{16,144},{24,152},{32,160},{40,168},{48,176},{56,1... | collective-permute-start | bytes 3145736 | tf_op jit(solution)/shard_map/ppermute | solution.py:578
  15.1 7.4 %copy-start = (bf16[16,3,256,128]{3,2,1,0:T(8,128)(2,1)S(1)}, bf16[16,3,256,128]{3,2,1,0:T(8,128)(2,1)}, u32[]{:S(2)}) copy-start(bf16[16,3,256,128]{3,2,1,0:T(8,128)(2,1)} %get-tuple-element.88._) | copy-start | bytes 9437188
  15.1 50.4 %all-to-all-start.3 = ((bf16[16,3,256,128]{3,2,1,0:T(8,128)(2,1)}), bf16[16,3,256,128]{3,2,1,0:T(8,128)(2,1)}, u32[]{:S(2)}, u32[]{:S(2)}) async-start(bf16[16,3,256,128]{3,2,1,0:T(8,128)(2,1)} %get-tuple-element.88._), calls=%async_computation.3 | async-start | bytes 6291456 | tf_op jit(solution)/shard_map/all_to_all | solution.py:575
  22.5 2.2 %copy-start.1 = (bf16[512,4096]{1,0:T(8,128)(2,1)S(1)}, bf16[512,4096]{1,0:T(8,128)(2,1)}, u32[]{:S(2)}) copy-start(bf16[512,4096]{1,0:T(8,128)(2,1)} %weight_ref.1) | copy-start | bytes 12582916
  24.6 15.3 %copy-start.14 = (s32[33]{0:T(128)S(1)}, s32[33]{0:T(128)}, u32[]{:S(2)}) copy-start(s32[33]{0:T(128)} %get-tuple-element.86.via_ref) | copy-start | bytes 400
  39.1 0.8 copy-start.2
  39.9 2.3 %collective-permute-start.2 = (f32[36,4096]{1,0:T(8,128)}, f32[36,4096]{1,0:T(8,128)S(1)}, u32[]{:S(2)}, u32[]{:S(2)}) collective-permute-start(f32[36,4096]{1,0:T(8,128)} %get-tuple-element.91), channel_id=1, source_target_pairs={{0,1},{1,0},{2,3},{3,2},{4,5},{5,4},{6,7},{7,6},{8,9},{9,8},{10,11... | collective-permute-start | bytes 1769480 | tf_op jit(solution)/shard_map/ppermute | solution.py:598
  43.7 48.5 %collective-permute-start.3 = (bf16[8,256,128]{2,1,0:T(8,128)(2,1)}, bf16[8,256,128]{2,1,0:T(8,128)(2,1)}, u32[]{:S(2)}, u32[]{:S(2)}) collective-permute-start(bf16[8,256,128]{2,1,0:T(8,128)(2,1)} %get-tuple-element.92), channel_id=1, source_target_pairs={{0,128},{8,136},{16,144},{24,152},{32,160},{40,168},{48,176},{56,1... | collective-permute-start | bytes 1572872 | tf_op jit(solution)/shard_map/ppermute | solution.py:578
  44.7 36.8 %collective-permute-start.6 = (bf16[3,3,4096]{2,1,0:T(4,128)(2,1)S(1)}, bf16[3,3,4096]{2,1,0:T(4,128)(2,1)S(1)}, u32[]{:S(2)}, u32[]{:S(2)}) collective-permute-start(bf16[3,3,4096]{2,1,0:T(4,128)(2,1)S(1)} %get-tuple-element.173), channel_id=1, source_target_pairs={{0,6},{1,7},{2,0},{3,1},{4,2},{5,3},{6,4},{7,5},{8,14},{9,15},{10,... | collective-permute-start | bytes 221192 | tf_op jit(solution)/shard_map/ppermute | solution.py:606
  45.2 41.2 %collective-permute-start.5 = (bf16[3,3,4096]{2,1,0:T(4,128)(2,1)S(1)}, bf16[3,3,4096]{2,1,0:T(4,128)(2,1)S(1)}, u32[]{:S(2)}, u32[]{:S(2)}) collective-permute-start(bf16[3,3,4096]{2,1,0:T(4,128)(2,1)S(1)} %get-tuple-element.174), channel_id=1, source_target_pairs={{0,4},{1,5},{2,6},{3,7},{4,0},{5,1},{6,2},{7,3},{8,12},{9,13},{10,... | collective-permute-start | bytes 221192 | tf_op jit(solution)/shard_map/ppermute | solution.py:606
  49.0 39.4 %collective-permute-start.4 = (bf16[3,3,4096]{2,1,0:T(4,128)(2,1)S(1)}, bf16[3,3,4096]{2,1,0:T(4,128)(2,1)}, u32[]{:S(2)}, u32[]{:S(2)}) collective-permute-start(bf16[3,3,4096]{2,1,0:T(4,128)(2,1)S(1)} %get-tuple-element.172), channel_id=1, source_target_pairs={{0,2},{1,3},{2,4},{3,5},{4,6},{5,7},{6,0},{7,1},{8,10},{9,11},{10,... | collective-permute-start | bytes 221192 | tf_op jit(solution)/shard_map/ppermute | solution.py:606
  65.5 33.7 %all-to-all-start.5 = ((bf16[16,2,256,128]{3,2,1,0:T(8,128)(2,1)}), bf16[16,2,256,128]{3,2,1,0:T(8,128)(2,1)S(1)}, u32[]{:S(2)}, u32[]{:S(2)}) async-start(bf16[16,2,256,128]{3,2,1,0:T(8,128)(2,1)} %relay_pages.7), calls=%async_computation.5 | async-start | bytes 4194304 | tf_op jit(solution)/shard_map/all_to_all | solution.py:575
  92.2 23.8 %collective-permute-start.8 = (bf16[2,3,256,128]{3,2,1,0:T(8,128)(2,1)}, bf16[2,3,256,128]{3,2,1,0:T(8,128)(2,1)S(1)}, u32[]{:S(2)}, u32[]{:S(2)}) collective-permute-start(bf16[2,3,256,128]{3,2,1,0:T(8,128)(2,1)} %lift_pages.1), channel_id=1, source_target_pairs={{0,128},{8,136},{16,144},{24,152},{32,160},{40,168},{48,176},{56,1... | collective-permute-start | bytes 1179656 | tf_op jit(solution)/shard_map/ppermute | solution.py:578
  99.2 1.3 %copy-start.7 = (bf16[16,2,256,128]{3,2,1,0:T(8,128)(2,1)}, bf16[16,2,256,128]{3,2,1,0:T(8,128)(2,1)S(1)}, u32[]{:S(2)}) copy-start(bf16[16,2,256,128]{3,2,1,0:T(8,128)(2,1)S(1)} %all-to-all-done.5.early_ref) | copy-start | bytes 6291460
  100.5 24.4 %all-to-all-start.4 = ((bf16[16,256,128]{2,1,0:T(8,128)(2,1)}), bf16[16,256,128]{2,1,0:T(8,128)(2,1)S(1)}, u32[]{:S(2)}, u32[]{:S(2)}) async-start(bf16[16,256,128]{2,1,0:T(8,128)(2,1)} %relay_pages.6), calls=%async_computation.4 | async-start | bytes 2097152 | tf_op jit(solution)/shard_map/all_to_all | solution.py:575
  116.0 0.8 copy-start.15
  125.0 1.0 copy-start.6

commit v3 on v2

--- a/solution.py
+++ b/solution.py
@@ -13,7 +13,7 @@
 STRAIGHT = 8
 LIFTED = 2
 RELAY_FIRST = 20.3
-RELAY_LAST = 20
+RELAY_LAST = 18
 PLACE_FIRST = 15
 ALL_VMEM = 62 * 2**20
 FREE = pl.CostEstimate(flops=0, bytes_accessed=0, transcendentals=0)
@@ -175,93 +175,11 @@
     return ((via_ref[source] >> place) & 1) == 1
 
 
-def first_pages_kernel(
-    me_ref,
-    own_ref,
-    cross_ref,
-    count_ref,
-    table_ref,
-    victim_ref,
-    dest_ref,
-    cache_ref,
-    early_ref,
-    via_ref,
-    held,
-    in_sem,
-    out_sem,
-):
-    count, pages = held.shape[:2]
-    groups = dest_ref.shape[1]
-    plane = groups // HALVES
-    straight = early_ref.shape[0]
-    group = me_ref[0]
-    my_half = group // plane
-
-    def page_in(j, p):
-        page = table_ref[p, victim_ref[0, j]]
-        return pltpu.make_async_copy(cache_ref.at[page], held.at[j, p], in_sem.at[j])
-
-    def copy_out(j, rank):
-        return pltpu.make_async_copy(held.at[j], early_ref.at[rank], out_sem)
-
-    def visit(act):
-        rank = jnp.int32(0)
-        for j in range(count):
-            target = dest_ref[j, group]
-            leaves = ((target // plane) != my_half) & jnp.logical_not(
-                goes_via(via_ref, group, target % plane)
-            )
-            leaves = leaves & (rank < straight)
-
-            @pl.when(leaves)
-            def _():
-                act(j, rank)
-
-            rank = rank + jnp.where(leaves, 1, 0)
-
-    def read(j, rank):
-        for p in range(pages):
-            page_in(j, p).start()
-
-    def write(j, rank):
-        for p in range(pages):
-            page_in(j, p).wait()
-        copy_out(j, rank).start()
-
-    bad = route(own_ref, cross_ref, count_ref, via_ref, my_half, plane, straight)
-    visit(read)
-    bad = bad | route(own_ref, cross_ref, count_ref, via_ref, 1 - my_half, plane, straight)
-    via_ref[groups] = bad
-    visit(write)
-    visit(lambda j, rank: copy_out(j, rank).wait())
-
-
-def first_pages(straight, me, masks, table, victims, dest, cache, pages):
-    count = victims.shape[1]
-    groups = dest.shape[1]
-    smem = pl.BlockSpec(memory_space=pltpu.SMEM)
-    anywhere = pl.BlockSpec(memory_space=pl.ANY)
-    return pl.pallas_call(
-        first_pages_kernel,
-        out_shape=(
-            jax.ShapeDtypeStruct((straight, pages) + cache.shape[1:], cache.dtype),
-            jax.ShapeDtypeStruct((groups + 1,), jnp.int32),
-        ),
-        in_specs=[smem] * 7 + [anywhere],
-        out_specs=(anywhere, smem),
-        scratch_shapes=[
-            pltpu.VMEM((count, pages) + cache.shape[1:], cache.dtype),
-            pltpu.SemaphoreType.DMA((count,)),
-            pltpu.SemaphoreType.DMA,
-        ],
-        cost_estimate=FREE,
-        name="first_pages",
-    )(me, *masks, table, victims, dest, cache)
-
-
 def pack_kernel(
     me_ref,
-    via_ref,
+    own_mask_ref,
+    cross_mask_ref,
+    count_ref,
     length_ref,
     table_ref,
     victim_ref,
@@ -269,9 +187,10 @@
     plan_ref,
     fresh_ref,
     cache_ref,
-    _,
+    via_ref,
+    early_ref,
+    late_ref,
     own_ref,
-    late_ref,
     held,
     in_sem,
     out_sem,
@@ -279,6 +198,7 @@
     count, pages, rows, _ = held.shape
     steps = fresh_ref.shape[0]
     page_len = rows // 2
+    groups = dest_ref.shape[1]
     plane = own_ref.shape[0]
     straight = late_ref.shape[0]
     group = me_ref[0]
@@ -300,6 +220,11 @@
 
         @pl.when(leaves)
         def _():
+            act(
+                pltpu.make_async_copy(
+                    held.at[j, pl.ds(0, pages - 1)], early_ref.at[rank], out_sem
+                )
+            )
             act(pltpu.make_async_copy(held.at[j, pages - 1], late_ref.at[rank], out_sem))
 
         return rank + jnp.where(leaves, 1, 0)
@@ -307,6 +232,9 @@
     for j in range(count):
         for p in range(pages):
             page_in(j, p).start()
+    masks = (own_mask_ref, cross_mask_ref, count_ref, via_ref)
+    bad = route(*masks, my_half, plane, straight)
+    via_ref[groups] = bad | route(*masks, 1 - my_half, plane, straight)
     row_ids = lax.broadcasted_iota(jnp.int32, (page_len, HEAD_SIZE), 0)
     rank = jnp.int32(0)
     for j in range(count):
@@ -331,8 +259,9 @@
         rank = send(j, rank, lambda copy: copy.wait())
 
 
-def pack(straight, scalars, fresh, cache, plane, early):
-    count = scalars[4].shape[1]
+def pack(straight, scalars, fresh, cache, plane):
+    dest = scalars[7]
+    count, groups = dest.shape
     steps = fresh.shape[0]
     rows, width = cache.shape[1:]
     smem = pl.BlockSpec(memory_space=pltpu.SMEM)
@@ -340,11 +269,13 @@
     return pl.pallas_call(
         pack_kernel,
         out_shape=(
+            jax.ShapeDtypeStruct((groups + 1,), jnp.int32),
+            jax.ShapeDtypeStruct((straight, steps - 1, rows, width), cache.dtype),
+            jax.ShapeDtypeStruct((straight, rows, width), cache.dtype),
             jax.ShapeDtypeStruct((plane, steps, rows, width), cache.dtype),
-            jax.ShapeDtypeStruct((straight, rows, width), cache.dtype),
         ),
-        in_specs=[smem] * 7 + [pl.BlockSpec(memory_space=pltpu.VMEM), anywhere, anywhere],
-        out_specs=(anywhere,) * 2,
+        in_specs=[smem] * 9 + [pl.BlockSpec(memory_space=pltpu.VMEM), anywhere],
+        out_specs=(smem,) + (anywhere,) * 3,
         scratch_shapes=[
             pltpu.VMEM((count, steps, rows, width), cache.dtype),
             pltpu.SemaphoreType.DMA((count,)),
@@ -352,7 +283,7 @@
         ],
         cost_estimate=FREE,
         name="pack_pages",
-    )(*scalars, fresh, cache, early)
+    )(*scalars, fresh, cache)
 
 
 def relay_kernel(me_ref, via_ref, dest_ref, got_ref, slots_ref, sem):
@@ -577,12 +508,9 @@
     def swap(slots):
         return lax.ppermute(slots, "grp", swap_halves)
 
-    def pack_args(via):
-        return (me, via, lengths, table, victims, dest, plan)
-
-    early, via = first_pages(STRAIGHT, me, masks, table, victims, dest, pages, steps_total - 1)
+    scalars = (me, *masks, lengths, table, victims, dest, plan)
+    via, early, late, own = pack(STRAIGHT, scalars, fresh_steps, pages, plane)
     early_got = swap(early)
-    own, late = pack(STRAIGHT, pack_args(via), fresh_steps, pages, plane, early)
     own_got = in_half(own)
     kept, given = attend(
         core.astype(jnp.int32)[None],
@@ -597,34 +525,32 @@
     )
     on_chip = kept + lax.ppermute(given, "tp", swap_cores)
     on_chip = on_chip.reshape(chips, -1, steps_total, on_chip.shape[1])
-    late, on_chip = lax.optimization_barrier((late, on_chip))
+    late, early_got, on_chip = lax.optimization_barrier((late, early_got, on_chip))
     late_got = swap(late)
-    projected = lax.dynamic_index_in_dim(on_chip, chip, 0, keepdims=False)
+    own_share = lax.dynamic_index_in_dim(on_chip, chip, 0, keepdims=False)
     on_chip = on_chip.astype(jnp.bfloat16)
+    shares = []
     for shift in range(1, chips):
         share = lax.dynamic_index_in_dim(on_chip, (chip + shift) % chips, 0, keepdims=False)
-        share = lax.ppermute(
-            share, "tp", [(r, (r + 2 * shift) % ranks) for r in range(ranks)]
+        shares.append(
+            lax.ppermute(share, "tp", [(r, (r + 2 * shift) % ranks) for r in range(ranks)])
         )
-        projected = projected + share.astype(jnp.float32)
-    projected = projected.astype(jnp.bfloat16)
 
     early_slots = relay(me, via, dest, early_got, plane, RELAY_FIRST)
     early_arrived = in_half(early_slots)
     lifted = lift(me, via, own_got)
-    lifted, late_got, projected = lax.optimization_barrier((lifted, late_got, projected))
     lifted_got = swap(lifted)
+    late_got, _ = lax.optimization_barrier((late_got, lifted))
     migrated = place_first(me, via, sources, own_got, early_arrived, lifted_got)
     late_slots = relay(me, via, dest, late_got, plane, RELAY_LAST)
     late_arrived = in_half(late_slots)
+    shares, _ = lax.optimization_barrier((shares, lifted_got))
+    projected = own_share + sum(share.astype(jnp.float32) for share in shares)
+    projected = projected.astype(jnp.bfloat16)
     migrated = place_late(me, via, sources, late_arrived, migrated)
 
     def straight_only(carry):
-        no_via = jnp.zeros_like(via)
-        early, _ = first_pages(
-            victim_count, me, masks, table, victims, dest, pages, steps_total - 1
-        )
-        own, late = pack(victim_count, pack_args(no_via), fresh_steps, pages, plane, early)
+        no_via, early, late, own = pack(victim_count, scalars, fresh_steps, pages, plane)
         own_got = in_half(own)
         early_arrived = in_half(relay(me, no_via, dest, swap(early), plane, 0))
         late_arrived = in_half(relay(me, no_via, dest, swap(late), plane, 0))

time: 130 us -> 128 us (0.985)
  the two profiles are of different devices: /device:TPU:64 before, /device:TPU:32 now
where the time goes in v3:
time: 128 us; the launch traced here: 127 us
  waiting for transfers between devices  48 us (38%)
  starting transfers between devices  33.4 us (26%)
  Pallas kernels  32.1 us (25%)
  local copies, waits for them, and re-layouts  7.98 us (6%)
  other arithmetic  3.88 us (3%)
    ppermute x3, waiting for transfers between devices, swap(): return lax.ppermute(slots, 'grp', swap_halves)  24.7 us
    all_to_all x3, waiting for transfers between devices, in_half(): lax.all_to_all(slots, 'grp', 0, 0, axis_index_groups=half_groups, tiled=T...  21.6 us
    all_to_all x3, starting transfers between devices, in_half(): lax.all_to_all(slots, 'grp', 0, 0, axis_index_groups=half_groups, tiled=T...  18.3 us
    pallas_call x1, Pallas kernels, attend(): pl.pallas_call(functools.partial(attend_kernel, requests // ranks), out_s...  14.4 us
    ppermute x3, starting transfers between devices, swap(): return lax.ppermute(slots, 'grp', swap_halves)  12.1 us
    unnamed x25, local copies, waits for them, and re-layouts  6.2 us
    pallas_call x1, Pallas kernels, pack(): pl.pallas_call(pack_kernel, out_shape=(jax.ShapeDtypeStruct((groups + 1,)...  4.73 us
    pallas_call x2, Pallas kernels, relay(): pl.pallas_call(relay_kernel, out_shape=jax.ShapeDtypeStruct((plane,) + go...  4.23 us
  transfers between devices with their start and end apart: 10, of which 5 were waited for; matrix products, arithmetic and copies ran while one was open for 4% of the time, Pallas kernels for 20%

profile of v3, /device:TPU:32, one launch (start us, length us, event | category | flops | bytes accessed | tf_op | source)
XLA Modules:
  0.0 127.0 jit_solution(12584601604949520951)
XLA Ops:
  0.6 0.8 copy.28
  1.5 0.8 select_reduce_fusion.1
  2.3 4.7 %pack_pages.3 = (s32[33]{0:T(128)}, bf16[8,2,256,128]{3,2,1,0:T(8,128)(2,1)}, bf16[8,256,128]{2,1,0:T(8,128)(2,1)}, bf16[16,3,256,128]{3,2,1,0:T(8,128)(2,1)}) custom-call(s32[1]{0:T(128)} %bitcast.me_ref, s32[32]{0:T(128)S(1)} %get-tuple-element.199.own_mask_ref, s32[32]{0:T(128)S(1)} %get-tuple-element.200.cross_mask_ref, ...), custom_call_target="tpu_custom_call" | custom-call | tf_op jit(solution)/shard_map/pack_pages/pallas_call | solution.py:269
  7.0 6.4 %collective-permute-start.2 = (bf16[8,2,256,128]{3,2,1,0:T(8,128)(2,1)}, bf16[8,2,256,128]{3,2,1,0:T(8,128)(2,1)}, u32[]{:S(2)}, u32[]{:S(2)}) collective-permute-start(bf16[8,2,256,128]{3,2,1,0:T(8,128)(2,1)} %get-tuple-element.90), channel_id=1, source_target_pairs={{0,128},{8,136},{16,144},{24,152},{32,160},{40,168},{48,176},{56,1... | collective-permute-start | bytes 3145736 | tf_op jit(solution)/shard_map/ppermute | solution.py:509
  13.4 7.4 %all-to-all-start.3 = ((bf16[16,3,256,128]{3,2,1,0:T(8,128)(2,1)}), bf16[16,3,256,128]{3,2,1,0:T(8,128)(2,1)}, u32[]{:S(2)}, u32[]{:S(2)}) async-start(bf16[16,3,256,128]{3,2,1,0:T(8,128)(2,1)} %get-tuple-element.91._), calls=%async_computation.3 | async-start | bytes 6291456 | tf_op jit(solution)/shard_map/all_to_all | solution.py:506
  21.0 2.2 %copy-done.1 = bf16[512,4096]{1,0:T(8,128)(2,1)S(1)} copy-done((bf16[512,4096]{1,0:T(8,128)(2,1)S(1)}, bf16[512,4096]{1,0:T(8,128)(2,1)}, u32[]{:S(2)}) %copy-start.1) | copy-done | bytes 4194328
  23.2 14.4 %attend_and_project.1 = (f32[36,4096]{1,0:T(8,128)S(1)}, f32[36,4096]{1,0:T(8,128)}) custom-call(s32[1]{0:T(128)} %bitcast.8.core_ref, s32[1,24]{1,0:T(1,128)S(1)} %copy-done.11, s32[4,24]{1,0:T(4,128)S(1)} %bitcast.58, bf16[24,16,128]{2,1,0:T(8,128)(2,1)S(1)} %pad.4.query_ref, bf16[24,2,3,128]{3,2,1,0:T(4,128)(2,1)S(1)} %bitcast.44, ...), custom_call_target="tpu_custom_call" | custom-call | tf_op jit(solution)/shard_map/attend_and_project/pallas_call | solution.py:132
  37.6 0.8 copy-done.2
  38.5 0.6 slice.3
  39.1 1.7 %collective-permute-done.3 = f32[36,4096]{1,0:T(8,128)S(1)} collective-permute-done((f32[36,4096]{1,0:T(8,128)}, f32[36,4096]{1,0:T(8,128)S(1)}, u32[]{:S(2)}, u32[]{:S(2)}) %collective-permute-start.3) | collective-permute-done | bytes 589856 | tf_op jit(solution)/shard_map/ppermute | solution.py:526
  40.8 1.2 add.65
  41.9 0.3 reshape.35
  42.2 17.4 %collective-permute-done.2.got_ref = bf16[8,2,256,128]{3,2,1,0:T(8,128)(2,1)} collective-permute-done((bf16[8,2,256,128]{3,2,1,0:T(8,128)(2,1)}, bf16[8,2,256,128]{3,2,1,0:T(8,128)(2,1)}, u32[]{:S(2)}, u32[]{:S(2)}) %collective-permute-start.2) | collective-permute-done | bytes 1048608 | tf_op jit(solution)/shard_map/ppermute | solution.py:509
  59.6 5.5 %collective-permute-start.8 = (bf16[8,256,128]{2,1,0:T(8,128)(2,1)}, bf16[8,256,128]{2,1,0:T(8,128)(2,1)}, u32[]{:S(2)}, u32[]{:S(2)}) collective-permute-start(bf16[8,256,128]{2,1,0:T(8,128)(2,1)} %get-tuple-element.99), channel_id=1, source_target_pairs={{0,128},{8,136},{16,144},{24,152},{32,160},{40,168},{48,176},{56,1... | collective-permute-start | bytes 1572872 | tf_op jit(solution)/shard_map/ppermute | solution.py:509
  65.1 2.3 %relay_pages.7 = bf16[16,2,256,128]{3,2,1,0:T(8,128)(2,1)} custom-call(s32[1]{0:T(128)} %bitcast.me_ref, s32[33]{0:T(128)} %get-tuple-element.95.via_ref, s32[16,32]{1,0:T(8,128)S(1)} %bitcast.50, bf16[8,2,256,128]{3,2,1,0:T(8,128)(2,1)} %collective-permute-done.2.got_ref), custom_call_target="tpu_custom_call" | custom-call | flops 20299999232 | tf_op jit(solution)/shard_map/relay_pages/pallas_call | solution.py:323
  67.6 7.1 %all-to-all-start.5 = ((bf16[16,2,256,128]{3,2,1,0:T(8,128)(2,1)}), bf16[16,2,256,128]{3,2,1,0:T(8,128)(2,1)S(1)}, u32[]{:S(2)}, u32[]{:S(2)}) async-start(bf16[16,2,256,128]{3,2,1,0:T(8,128)(2,1)} %relay_pages.7), calls=%async_computation.5 | async-start | bytes 4194304 | tf_op jit(solution)/shard_map/all_to_all | solution.py:506
  74.7 0.8 dynamic-slice_bitcast_fusion
  75.5 0.8 collective-permute-start.4
  76.2 2.2 %collective-permute-start.5 = (bf16[3,3,4096]{2,1,0:T(4,128)(2,1)}, bf16[3,3,4096]{2,1,0:T(4,128)(2,1)}, u32[]{:S(2)}, u32[]{:S(2)}) collective-permute-start(bf16[3,3,4096]{2,1,0:T(4,128)(2,1)} %get-tuple-element.178), channel_id=1, source_target_pairs={{0,4},{1,5},{2,6},{3,7},{4,0},{5,1},{6,2},{7,3},{8,12},{9,13},{10,... | collective-permute-start | bytes 221192 | tf_op jit(solution)/shard_map/ppermute | solution.py:536
  78.4 2.6 %lift_pages.1 = bf16[2,3,256,128]{3,2,1,0:T(8,128)(2,1)} custom-call(s32[1]{0:T(128)} %bitcast.me_ref, s32[33]{0:T(128)} %get-tuple-element.95.via_ref, bf16[16,3,256,128]{3,2,1,0:T(8,128)(2,1)} %all-to-all-done.3.own_ref), custom_call_target="tpu_custom_call" | custom-call | tf_op jit(solution)/shard_map/lift_pages/pallas_call | solution.py:358
  81.1 0.2 collective-permute-start.7
  81.3 7.3 %collective-permute-done.8.got_ref = bf16[8,256,128]{2,1,0:T(8,128)(2,1)} collective-permute-done((bf16[8,256,128]{2,1,0:T(8,128)(2,1)}, bf16[8,256,128]{2,1,0:T(8,128)(2,1)}, u32[]{:S(2)}, u32[]{:S(2)}) %collective-permute-start.8) | collective-permute-done | bytes 524320 | tf_op jit(solution)/shard_map/ppermute | solution.py:509
  88.6 1.9 %relay_pages.6 = bf16[16,256,128]{2,1,0:T(8,128)(2,1)} custom-call(s32[1]{0:T(128)} %bitcast.me_ref, s32[33]{0:T(128)} %get-tuple-element.95.via_ref, s32[16,32]{1,0:T(8,128)S(1)} %bitcast.51, bf16[8,256,128]{2,1,0:T(8,128)(2,1)} %collective-permute-done.8.got_ref), custom_call_target="tpu_custom_call" | custom-call | flops 17999998976 | tf_op jit(solution)/shard_map/relay_pages/pallas_call | solution.py:323
  90.5 12.7 %all-to-all-done.5.early_ref = bf16[16,2,256,128]{3,2,1,0:T(8,128)(2,1)S(1)} async-done(((bf16[16,2,256,128]{3,2,1,0:T(8,128)(2,1)}), bf16[16,2,256,128]{3,2,1,0:T(8,128)(2,1)S(1)}, u32[]{:S(2)}, u32[]{:S(2)}) %all-to-all-start.5) | async-done | bytes 2097184 | tf_op jit(solution)/shard_map/all_to_all | solution.py:506
  103.2 1.4 %copy-done.7 = bf16[16,2,256,128]{3,2,1,0:T(8,128)(2,1)} copy-done((bf16[16,2,256,128]{3,2,1,0:T(8,128)(2,1)}, bf16[16,2,256,128]{3,2,1,0:T(8,128)(2,1)S(1)}, u32[]{:S(2)}) %copy-start.7) | copy-done | bytes 2097176
  104.5 3.9 %all-to-all-start.4 = ((bf16[16,256,128]{2,1,0:T(8,128)(2,1)}), bf16[16,256,128]{2,1,0:T(8,128)(2,1)S(1)}, u32[]{:S(2)}, u32[]{:S(2)}) async-start(bf16[16,256,128]{2,1,0:T(8,128)(2,1)} %relay_pages.6), calls=%async_computation.4 | async-start | bytes 2097152 | tf_op jit(solution)/shard_map/all_to_all | solution.py:506
  108.4 4.1 %place_first.3._ = bf16[16,3,256,128]{3,2,1,0:T(8,128)(2,1)} custom-call(s32[1]{0:T(128)} %bitcast.me_ref, s32[33]{0:T(128)} %get-tuple-element.95.via_ref, s32[16]{0:T(128)S(1)} %get-tuple-element.209.source_ref, bf16[16,3,256,128]{3,2,1,0:T(8,128)(2,1)} %all-to-all-done.3.own_ref, bf16[16,2,256,128]{3,2,1,0:T(8,128)(2,1)} %copy-done.7, ...), custom_call_target="tpu_custom_call" | custom-call | flops 15000000512 | tf_op jit(solution)/shard_map/place_first/pallas_call | solution.py:436
  112.5 1.7 %fusion.1 = bf16[1,3,3,4096]{3,2,1,0:T(4,128)(2,1)} fusion(bf16[3,3,4096]{2,1,0:T(4,128)(2,1)} %collective-permute-done.6, bf16[3,3,4096]{2,1,0:T(4,128)(2,1)} %collective-permute-done.5, bf16[3,3,4096]{2,1,0:T(4,128)(2,1)} %collective-permute-done.4, f32[4,3,3,4096]{3,2,1,0:T(4,128)S(1)} %reshape.35, s32[]{:T(128)S(6)} %select_n.76), kind=kLoop, calls=%fused_computation.2 | loop fusion | flops 258048 | bytes 442372 | tf_op jit(solution)/shard_map/broadcast_in_dim | solution.py:563
  114.3 8.9 %all-to-all-done.4.late_ref = bf16[16,256,128]{2,1,0:T(8,128)(2,1)S(1)} async-done(((bf16[16,256,128]{2,1,0:T(8,128)(2,1)}), bf16[16,256,128]{2,1,0:T(8,128)(2,1)S(1)}, u32[]{:S(2)}, u32[]{:S(2)}) %all-to-all-start.4) | async-done | bytes 1048608 | tf_op jit(solution)/shard_map/all_to_all | solution.py:506
  123.2 1.0 copy-done.5
  124.2 2.0 %place_late.3 = bf16[16,3,256,128]{3,2,1,0:T(8,128)(2,1)} custom-call(s32[1]{0:T(128)} %bitcast.me_ref, s32[33]{0:T(128)} %get-tuple-element.95.via_ref, s32[16]{0:T(128)S(1)} %get-tuple-element.209.source_ref, bf16[16,256,128]{2,1,0:T(8,128)(2,1)} %copy-done.5, bf16[16,3,256,128]{3,2,1,0:T(8,128)(2,1)} %place_first.3._), custom_call_target="tpu_custom_call", output_to_operand_aliasing={{}: (4, {})} | custom-call | tf_op jit(solution)/shard_map/place_late/pallas_call | solution.py:451
  126.2 0.6 while.9
  (34 shorter events, 0.3 us)
Async XLA Ops:
  7.0 52.6 %collective-permute-start.2 = (bf16[8,2,256,128]{3,2,1,0:T(8,128)(2,1)}, bf16[8,2,256,128]{3,2,1,0:T(8,128)(2,1)}, u32[]{:S(2)}, u32[]{:S(2)}) collective-permute-start(bf16[8,2,256,128]{3,2,1,0:T(8,128)(2,1)} %get-tuple-element.90), channel_id=1, source_target_pairs={{0,128},{8,136},{16,144},{24,152},{32,160},{40,168},{48,176},{56,1... | collective-permute-start | bytes 3145736 | tf_op jit(solution)/shard_map/ppermute | solution.py:509
  13.4 7.4 %copy-start.10 = (bf16[3,1,24,512]{3,2,1,0:T(8,128)(2,1)S(1)}, bf16[3,1,24,512]{3,2,1,0:T(8,128)(2,1)}, u32[]{:S(2)}) copy-start(bf16[3,1,24,512]{3,2,1,0:T(8,128)(2,1)} %param.11) | copy-start | bytes 221188
  13.4 7.5 %copy-start = (bf16[16,3,256,128]{3,2,1,0:T(8,128)(2,1)S(1)}, bf16[16,3,256,128]{3,2,1,0:T(8,128)(2,1)}, u32[]{:S(2)}) copy-start(bf16[16,3,256,128]{3,2,1,0:T(8,128)(2,1)} %get-tuple-element.91._) | copy-start | bytes 9437188
  13.4 7.5 %copy-start.9 = (s32[1,24,4]{1,2,0:T(4,128)S(1)}, s32[1,24,4]{1,2,0:T(4,128)}, u32[]{:S(2)}) copy-start(s32[1,24,4]{1,2,0:T(4,128)} %param.16) | copy-start | bytes 1156
  13.4 7.5 %copy-start.11 = (s32[1,24]{1,0:T(1,128)S(1)}, s32[1,24]{1,0:T(1,128)}, u32[]{:S(2)}) copy-start(s32[1,24]{1,0:T(1,128)} %length_ref.3) | copy-start | bytes 292
  13.4 54.2 %all-to-all-start.3 = ((bf16[16,3,256,128]{3,2,1,0:T(8,128)(2,1)}), bf16[16,3,256,128]{3,2,1,0:T(8,128)(2,1)}, u32[]{:S(2)}, u32[]{:S(2)}) async-start(bf16[16,3,256,128]{3,2,1,0:T(8,128)(2,1)} %get-tuple-element.91._), calls=%async_computation.3 | async-start | bytes 6291456 | tf_op jit(solution)/shard_map/all_to_all | solution.py:506
  21.0 2.2 %copy-start.1 = (bf16[512,4096]{1,0:T(8,128)(2,1)S(1)}, bf16[512,4096]{1,0:T(8,128)(2,1)}, u32[]{:S(2)}) copy-start(bf16[512,4096]{1,0:T(8,128)(2,1)} %weight_ref.1) | copy-start | bytes 12582916
  23.2 15.3 %copy-start.13 = (s32[33]{0:T(128)S(1)}, s32[33]{0:T(128)}, u32[]{:S(2)}) copy-start(s32[33]{0:T(128)} %get-tuple-element.95.via_ref) | copy-start | bytes 400
  37.6 0.9 copy-start.2
  38.5 26.7 %copy-start.6 = (s32[32,16]{0,1:T(8,128)S(1)}, s32[32,16]{0,1:T(8,128)}, u32[]{:S(2)}) copy-start(s32[32,16]{0,1:T(8,128)} %param.18) | copy-start | bytes 6148
  38.5 2.3 %collective-permute-start.3 = (f32[36,4096]{1,0:T(8,128)}, f32[36,4096]{1,0:T(8,128)S(1)}, u32[]{:S(2)}, u32[]{:S(2)}) collective-permute-start(f32[36,4096]{1,0:T(8,128)} %get-tuple-element.93), channel_id=1, source_target_pairs={{0,1},{1,0},{2,3},{3,2},{4,5},{5,4},{6,7},{7,6},{8,9},{9,8},{10,11... | collective-permute-start | bytes 1769480 | tf_op jit(solution)/shard_map/ppermute | solution.py:526
  59.6 28.9 %collective-permute-start.8 = (bf16[8,256,128]{2,1,0:T(8,128)(2,1)}, bf16[8,256,128]{2,1,0:T(8,128)(2,1)}, u32[]{:S(2)}, u32[]{:S(2)}) collective-permute-start(bf16[8,256,128]{2,1,0:T(8,128)(2,1)} %get-tuple-element.99), channel_id=1, source_target_pairs={{0,128},{8,136},{16,144},{24,152},{32,160},{40,168},{48,176},{56,1... | collective-permute-start | bytes 1572872 | tf_op jit(solution)/shard_map/ppermute | solution.py:509
  67.6 35.5 %all-to-all-start.5 = ((bf16[16,2,256,128]{3,2,1,0:T(8,128)(2,1)}), bf16[16,2,256,128]{3,2,1,0:T(8,128)(2,1)S(1)}, u32[]{:S(2)}, u32[]{:S(2)}) async-start(bf16[16,2,256,128]{3,2,1,0:T(8,128)(2,1)} %relay_pages.7), calls=%async_computation.5 | async-start | bytes 4194304 | tf_op jit(solution)/shard_map/all_to_all | solution.py:506
  75.5 37.0 %collective-permute-start.4 = (bf16[3,3,4096]{2,1,0:T(4,128)(2,1)}, bf16[3,3,4096]{2,1,0:T(4,128)(2,1)}, u32[]{:S(2)}, u32[]{:S(2)}) collective-permute-start(bf16[3,3,4096]{2,1,0:T(4,128)(2,1)} %get-tuple-element.179), channel_id=1, source_target_pairs={{0,2},{1,3},{2,4},{3,5},{4,6},{5,7},{6,0},{7,1},{8,10},{9,11},{10,... | collective-permute-start | bytes 221192 | tf_op jit(solution)/shard_map/ppermute | solution.py:536
  76.2 36.3 %collective-permute-start.5 = (bf16[3,3,4096]{2,1,0:T(4,128)(2,1)}, bf16[3,3,4096]{2,1,0:T(4,128)(2,1)}, u32[]{:S(2)}, u32[]{:S(2)}) collective-permute-start(bf16[3,3,4096]{2,1,0:T(4,128)(2,1)} %get-tuple-element.178), channel_id=1, source_target_pairs={{0,4},{1,5},{2,6},{3,7},{4,0},{5,1},{6,2},{7,3},{8,12},{9,13},{10,... | collective-permute-start | bytes 221192 | tf_op jit(solution)/shard_map/ppermute | solution.py:536
  78.4 34.1 %collective-permute-start.6 = (bf16[3,3,4096]{2,1,0:T(4,128)(2,1)S(1)}, bf16[3,3,4096]{2,1,0:T(4,128)(2,1)}, u32[]{:S(2)}, u32[]{:S(2)}) collective-permute-start(bf16[3,3,4096]{2,1,0:T(4,128)(2,1)S(1)} %get-tuple-element.177), channel_id=1, source_target_pairs={{0,6},{1,7},{2,0},{3,1},{4,2},{5,3},{6,4},{7,5},{8,14},{9,15},{10,... | collective-permute-start | bytes 221192 | tf_op jit(solution)/shard_map/ppermute | solution.py:536
  81.1 27.4 %collective-permute-start.7 = (bf16[2,3,256,128]{3,2,1,0:T(8,128)(2,1)}, bf16[2,3,256,128]{3,2,1,0:T(8,128)(2,1)}, u32[]{:S(2)}, u32[]{:S(2)}) collective-permute-start(bf16[2,3,256,128]{3,2,1,0:T(8,128)(2,1)} %lift_pages.1), channel_id=1, source_target_pairs={{0,128},{8,136},{16,144},{24,152},{32,160},{40,168},{48,176},{56,1... | collective-permute-start | bytes 1179656 | tf_op jit(solution)/shard_map/ppermute | solution.py:509
  103.2 1.4 %copy-start.7 = (bf16[16,2,256,128]{3,2,1,0:T(8,128)(2,1)}, bf16[16,2,256,128]{3,2,1,0:T(8,128)(2,1)S(1)}, u32[]{:S(2)}) copy-start(bf16[16,2,256,128]{3,2,1,0:T(8,128)(2,1)S(1)} %all-to-all-done.5.early_ref) | copy-start | bytes 6291460
  104.5 18.7 %all-to-all-start.4 = ((bf16[16,256,128]{2,1,0:T(8,128)(2,1)}), bf16[16,256,128]{2,1,0:T(8,128)(2,1)S(1)}, u32[]{:S(2)}, u32[]{:S(2)}) async-start(bf16[16,256,128]{2,1,0:T(8,128)(2,1)} %relay_pages.6), calls=%async_computation.4 | async-start | bytes 2097152 | tf_op jit(solution)/shard_map/all_to_all | solution.py:506
  114.3 12.0 %copy-start.8 = (s32[32,16,3]{0,1,2:T(8,128)S(1)}, s32[32,16,3]{0,1,2:T(8,128)}, u32[]{:S(2)}) copy-start(s32[32,16,3]{0,1,2:T(8,128)} %param.19) | copy-start | bytes 18436
  114.3 12.0 %copy-start.12 = (s32[1,16]{1,0:T(1,128)S(1)}, s32[1,16]{1,0:T(1,128)}, u32[]{:S(2)}) copy-start(s32[1,16]{1,0:T(1,128)} %victim_ref.1) | copy-start | bytes 196
  123.2 1.0 copy-start.5
